TPU v7x, 32 devices: a whole 2x2x4 slice. The times are simulated.
32 devices in a mesh: rep: 4 (over z), grp: 8 (over y, x, core).
Axes of the slice: x: 2, y: 2, z: 4, core: 2. Of those that a mesh axis runs over, the one named last changes fastest.
Arguments:
- tokens: bfloat16 [192, 197, 768], P(('rep', 'grp')), may hold values from -6 to 6
- cotangent: bfloat16 [192, 197, 768], P(('rep', 'grp')), may hold values from -6 to 6
- heads_in: bfloat16 [768, 2304], P('grp'), may hold values from -0.3125 to 0.3125
- heads_out: bfloat16 [768, 768], P('grp'), may hold values from -0.875 to 0.875
- slot_router: bfloat16 [768, 4], P('grp'), may hold values from -0.109375 to 0.109375
- first_gain: bfloat16 [768], P('grp'), may hold values from 0.5 to 1.5
- second_gain: bfloat16 [768], P('grp'), may hold values from 0.5 to 1.5
- expert_in: bfloat16 [8, 768, 1536], P('grp'), may hold values from -3 to 3
- expert_out: bfloat16 [8, 1536, 768], P('grp'), may hold values from -0.21875 to 0.21875
Outputs:
- output: bfloat16 [192, 197, 768], P(('rep', 'grp'))
- token_grad: bfloat16 [192, 197, 768], P(('rep', 'grp'))
- heads_in_grad: float32 [768, 2304], P('grp')
- heads_out_grad: float32 [768, 768], P('grp')
- router_grad: float32 [768, 4], P('grp')
- first_gain_grad: float32 [768], P('grp')
- second_gain_grad: float32 [768], P('grp')
- expert_in_grad: float32 [8, 768, 1536], P('grp')
- expert_out_grad: float32 [8, 1536, 768], P('grp')
All inputs are finite; a program needn't handle non-finite values.
Results may differ from a plain program's by a relative error of at most 0.019.
Values may be sent and summed in bfloat16 or wider, within the bound.
No kernel may reach another device: no remote copies, remote signals or barrier semaphores. Data moves between devices by JAX's collectives and lax.ppermute only.
A program may use at most 192 MiB of HBM per device.

v0:
```python
import functools

import jax
import jax.numpy as jnp
from jax import lax
from jax.experimental import pallas as pl
from jax.experimental.pallas import tpu as pltpu
from jax.sharding import PartitionSpec as P

HEADS = 12
LANES = 128
F32 = jnp.float32
BF16 = jnp.bfloat16
LOW = -1e30
VMEM_BYTES = 56 * 1024 * 1024

NN = (((1,), (0,)), ((), ()))
NT = (((1,), (1,)), ((), ()))
TN = (((0,), (0,)), ((), ()))


def dot(left, right, form=NN):
    return lax.dot_general(left, right, form, preferred_element_type=F32)


def swap(values, axis, size, bit):
    return lax.ppermute(values, axis, [(place, place ^ bit) for place in range(size)])


def bits_of(size):
    bit, bits = 1, []
    while bit < size:
        bits.append(bit)
        bit *= 2
    return bits


def flip_blocks(blocks, place):
    size = blocks.shape[0]
    for bit in bits_of(size):
        pairs = blocks.reshape((size // (2 * bit), 2, bit) + blocks.shape[1:])
        odd = (place & bit) > 0
        low, high = pairs[:, 0], pairs[:, 1]
        pairs = jnp.stack([jnp.where(odd, high, low), jnp.where(odd, low, high)], axis=1)
        blocks = pairs.reshape(blocks.shape)
    return blocks


def gather_part(values, bits, size):
    held = values[None]
    order = [0]
    for bit in bits:
        held = jnp.concatenate([held, swap(held, "grp", size, bit)])
        order = order + [place ^ bit for place in order]
    return jnp.stack([held[order.index(place)] for place in sorted(order)])


def gather_rows(values, size):
    bits = bits_of(size)
    rows = values.shape[0]
    half = rows // 2
    first = gather_part(values[:half], bits[1:], size)
    second = gather_part(values[half:], bits[1:][::-1], size)
    both = jnp.concatenate([first, second], axis=1)
    other = swap(both, "grp", size, 1)
    return jnp.stack([both, other], axis=1).reshape(size, rows, -1)


def add_low(left, right):
    return (left.astype(F32) + right.astype(F32)).astype(BF16)


def halve(values, size, bits):
    for bit in bits:
        keep = [(p, v) for p, v in values if not p & bit]
        give = dict((p, v) for p, v in values if p & bit)
        sent = swap(jnp.stack([give[p | bit] for p, _ in keep]), "grp", size, bit)
        values = [(p, add_low(v, sent[i])) for i, (p, v) in enumerate(keep)]
    return values


def scatter_sum(relative, size):
    bits = bits_of(size)
    start = halve([(p, relative[p]) for p in range(size)], size, [1])
    cut = relative.shape[-1] // 256 * 128
    first = halve([(p, v[:, :cut]) for p, v in start], size, bits[1:])
    second = halve([(p, v[:, cut:]) for p, v in start], size, bits[1:][::-1])
    return jnp.concatenate([first[0][1], second[0][1]], axis=-1)


def sum_rep(values, size):
    total = values
    for bit in [1, 3] if size == 4 else bits_of(size):
        total = add_low(total, swap(total, "rep", size, bit))
    return total


def iota(shape, axis):
    return lax.broadcasted_iota(jnp.int32, shape, axis)


def normalize(values):
    center = values - jnp.mean(values, axis=-1, keepdims=True)
    factor = lax.rsqrt(jnp.mean(center * center, axis=-1, keepdims=True) + 1e-06)
    return center * factor, factor


def norm_back(grad_norm, gain, normed, factor):
    scaled = grad_norm * gain
    inner = (
        scaled
        - jnp.mean(scaled, axis=-1, keepdims=True)
        - normed * jnp.mean(scaled * normed, axis=-1, keepdims=True)
    )
    return factor * inner


def place_rows(order_ref, source_ref, target_ref):
    rows = source_ref.shape[1]
    for k in range(source_ref.shape[0]):
        start = pl.multiple_of(order_ref[k] * rows, 32)
        target_ref[pl.ds(start, rows), :] = source_ref[k]


def attend_body(first, places, order_ref, source_ref, gain_ref, w_ref, *refs):
    if first:
        act_ref, joint_ref, prob_ref, mixed_ref, weight = refs
    else:
        joint_ref, prob_ref, mixed_ref, weight = refs

    @pl.when(pl.program_id(0) == 0)
    def _():
        place_rows(order_ref, w_ref, weight)

    if first:
        normed, _ = normalize(source_ref[0].astype(F32))
        act = (normed * gain_ref[...]).astype(BF16)
        act_ref[0] = act
    else:
        act = source_ref[0]
    joint = dot(act, weight[...]).astype(BF16)
    joint_ref[0] = joint
    tall = act.shape[0]
    third = joint.shape[1] // 3
    low = iota((tall, LANES), 1) < LANES // 2
    inside = iota((tall, LANES), 0) < places
    seen = iota((tall, tall), 1) < places
    for pair in range(third // LANES):
        query, keys, values = (
            joint[:, part * third + pair * LANES : part * third + (pair + 1) * LANES]
            for part in range(3)
        )
        query = query * 0.125
        outs = []
        for side in range(2):
            mine = low if side == 0 else ~low
            scores = dot(jnp.where(mine, query, 0), keys, NT)
            scores = jnp.where(seen, scores, LOW)
            power = jnp.exp(scores - jnp.max(scores, axis=1, keepdims=True))
            prob = (power * (1.0 / jnp.sum(power, axis=1, keepdims=True))).astype(BF16)
            prob_ref[0, 2 * pair + side] = prob
            outs.append(dot(prob, values))
        mixed = jnp.where(inside, jnp.where(low, outs[0], outs[1]), 0.0)
        mixed_ref[0, :, pair * LANES : (pair + 1) * LANES] = mixed.astype(BF16)


def spec_image(shape):
    count = len(shape)
    return pl.BlockSpec((1,) + shape[1:], lambda i: (i,) + (0,) * (count - 1))


def spec_whole(shape):
    count = len(shape)
    return pl.BlockSpec(shape, lambda i: (0,) * count)


SMEM = pl.BlockSpec(memory_space=pltpu.SMEM)


def params():
    return pltpu.CompilerParams(vmem_limit_bytes=VMEM_BYTES)


def cost(flops, data):
    return pl.CostEstimate(flops=int(flops), bytes_accessed=int(data), transcendentals=0)


def attend(first, places, order, source, gain, w):
    images, tall, features = source.shape
    width = w.shape[-1]
    heads = width // 3 // 64
    shapes = [
        ((images, tall, width), BF16),
        ((images, heads, tall, tall), BF16),
        ((images, tall, width // 3), BF16),
    ]
    if first:
        shapes = [((images, tall, features), BF16)] + shapes
    return pl.pallas_call(
        functools.partial(attend_body, first, places),
        grid=(images,),
        in_specs=[SMEM, spec_image(source.shape), spec_whole(gain.shape), spec_whole(w.shape)],
        out_specs=[spec_image(s) for s, _ in shapes],
        out_shape=[jax.ShapeDtypeStruct(s, t) for s, t in shapes],
        scratch_shapes=[pltpu.VMEM((features, width), BF16)],
        compiler_params=params(),
        cost_estimate=cost(2 * images * tall * features * width * 3, 8e6),
        name="attend",
    )(order, source, gain, w)


def softmaxes(logits, places, experts):
    rows = iota(logits.shape, 0) < places
    lanes = iota(logits.shape, 1) < experts
    tall = jnp.where(rows, logits, LOW)
    tall = jnp.exp(tall - jnp.max(tall, axis=0, keepdims=True))
    dispatch = tall / jnp.sum(tall, axis=0, keepdims=True)
    wide = jnp.where(lanes, logits, LOW)
    wide = jnp.exp(wide - jnp.max(wide, axis=1, keepdims=True))
    combine = wide / jnp.sum(wide, axis=1, keepdims=True)
    return dispatch, combine


def route_body(
    places, experts, order_ref, token_ref, cot_ref, m0, m1, m2, w_ref, gain_ref, router_ref,
    resid_ref, logit_ref, packed_ref, weight,
):
    @pl.when(pl.program_id(0) == 0)
    def _():
        place_rows(order_ref, w_ref, weight)

    resid = token_ref[0].astype(F32)
    part = m0.shape[-1]
    for c, mixed in enumerate((m0, m1, m2)):
        resid = resid + dot(mixed[0], weight[c * part : (c + 1) * part, :])
    resid_ref[0] = resid
    normed, _ = normalize(resid)
    act = (normed * gain_ref[...]).astype(BF16)
    logits = dot(act, router_ref[...])
    logit_ref[0] = logits
    dispatch, combine = softmaxes(logits, places, experts)
    features = act.shape[1]
    rows = packed_ref.shape[1]
    packed_ref[0, :, :features] = dot(dispatch.astype(BF16), act, TN)[:rows].astype(BF16)
    packed_ref[0, :, features:] = dot(combine.astype(BF16), cot_ref[0], TN)[:rows].astype(BF16)


def route(places, experts, slot_rows, order, tokens, cot, mixed, w, gain, router):
    images, tall, features = tokens.shape
    shapes = [
        ((images, tall, features), F32),
        ((images, tall, LANES), F32),
        ((images, slot_rows, 2 * features), BF16),
    ]
    return pl.pallas_call(
        functools.partial(route_body, places, experts),
        grid=(images,),
        in_specs=[SMEM, spec_image(tokens.shape), spec_image(cot.shape)]
        + [spec_image(m.shape) for m in mixed]
        + [spec_whole(w.shape), spec_whole(gain.shape), spec_whole(router.shape)],
        out_specs=[spec_image(s) for s, _ in shapes],
        out_shape=[jax.ShapeDtypeStruct(s, t) for s, t in shapes],
        scratch_shapes=[pltpu.VMEM((features, features), BF16)],
        compiler_params=params(),
        cost_estimate=cost(4 * images * tall * features * features, 8e6),
        name="route",
    )(order, tokens, cot, *mixed, w, gain, router)


def gelu_parts(values):
    scale, cubic = 0.7978845608028654, 0.044715
    square = values * values
    bent = jnp.tanh(scale * values * (1.0 + cubic * square))
    half = 0.5 * (1.0 + bent)
    slope = half + 0.5 * values * (1.0 - bent * bent) * scale * (1.0 + 3.0 * cubic * square)
    return values * half, slope


def expert_body(rows_ref, in_ref, out_ref, back_ref):
    features = in_ref.shape[0]
    rows, arriving = rows_ref[:, :features], rows_ref[:, features:]
    total = jnp.zeros((rows.shape[0], features), F32)
    grad_total = total
    step = 512
    for start in range(0, in_ref.shape[1], step):
        w_in = in_ref[:, start : start + step]
        w_out = out_ref[start : start + step, :]
        hidden, slope = gelu_parts(dot(rows, w_in))
        grad_pre = (dot(arriving, w_out, NT) * slope).astype(BF16)
        total = total + dot(hidden.astype(BF16), w_out)
        grad_total = grad_total + dot(grad_pre, w_in, NT)
    back_ref[:, :features] = total.astype(BF16)
    back_ref[:, features:] = grad_total.astype(BF16)


def expert(rows, piece_in, piece_out):
    return pl.pallas_call(
        expert_body,
        grid=(1,),
        in_specs=[spec_whole(rows.shape), spec_whole(piece_in.shape), spec_whole(piece_out.shape)],
        out_specs=spec_whole(rows.shape),
        out_shape=jax.ShapeDtypeStruct(rows.shape, BF16),
        compiler_params=params(),
        cost_estimate=cost(8 * 256 * piece_in.size, 5e6),
        name="expert",
    )(rows, piece_in, piece_out)


def expert_grad_body(rows_ref, in_ref, out_ref, grad_in_ref, grad_out_ref):
    features = in_ref.shape[0]
    rows, arriving = rows_ref[:, :features], rows_ref[:, features:]
    hidden, slope = gelu_parts(dot(rows, in_ref[...]))
    grad_pre = (dot(arriving, out_ref[...], NT) * slope).astype(BF16)
    grad_in_ref[...] = dot(rows, grad_pre, TN)
    grad_out_ref[...] = dot(hidden.astype(BF16), arriving, TN)


def expert_grad(rows, piece_in, piece_out):
    features, hidden = piece_in.shape
    step = 512
    wide = pl.BlockSpec((features, step), lambda i: (0, i))
    high = pl.BlockSpec((step, features), lambda i: (i, 0))
    return pl.pallas_call(
        expert_grad_body,
        grid=(hidden // step,),
        in_specs=[spec_whole(rows.shape), wide, high],
        out_specs=[wide, high],
        out_shape=[
            jax.ShapeDtypeStruct(piece_in.shape, F32),
            jax.ShapeDtypeStruct(piece_out.shape, F32),
        ],
        compiler_params=params(),
        cost_estimate=cost(8 * rows.shape[0] * piece_in.size, 14e6),
        name="expert_grad",
    )(rows, piece_in, piece_out)


def back_body(
    places, experts, order_ref, resid_ref, logit_ref, cot_ref, m0, m1, m2, summed_ref, w_ref, gain_ref,
    router_ref, output_ref, att_ref, grad_mixed_ref, grad_w_ref, weight, slots, total, side, gain_sum,
):
    step = pl.program_id(0)
    features = gain_ref.shape[1]

    @pl.when(step == 0)
    def _():
        place_rows(order_ref, w_ref, weight)
        slots[...] = jnp.zeros_like(slots)
        total[...] = jnp.zeros_like(total)
        side[...] = jnp.zeros_like(side)
        gain_sum[...] = jnp.zeros_like(gain_sum)

    rows = summed_ref.shape[1]
    slots[:rows, :] = summed_ref[0]
    expert_sum, grad_slots = slots[:, :features], slots[:, features:]
    resid = resid_ref[0]
    cot = cot_ref[0]
    gain = gain_ref[...]
    router = router_ref[...]
    dispatch, combine = softmaxes(logit_ref[0], places, experts)
    output = resid + dot(combine.astype(BF16), expert_sum)
    output_ref[0] = output[:places].astype(BF16)
    normed, factor = normalize(resid)
    act = (normed * gain).astype(BF16)
    grad_comb = dot(cot, expert_sum, NT)
    grad_disp = dot(act, grad_slots, NT)
    grad_logits = combine * (grad_comb - jnp.sum(grad_comb * combine, axis=1, keepdims=True))
    grad_logits = grad_logits + dispatch * (
        grad_disp - jnp.sum(grad_disp * dispatch, axis=0, keepdims=True)
    )
    grad_logits = grad_logits.astype(BF16)
    grad_act = dot(dispatch.astype(BF16), grad_slots) + dot(grad_logits, router, NT)
    side[...] += dot(act, grad_logits, TN)
    gain_sum[...] += jnp.sum(grad_act * normed, axis=0, keepdims=True)
    att = (cot.astype(F32) + norm_back(grad_act, gain, normed, factor)).astype(BF16)
    att_ref[0] = att
    grad_mixed_ref[0] = dot(att, weight[...], NT).astype(BF16)
    part = m0.shape[-1]
    for c, mixed in enumerate((m0, m1, m2)):
        total[c * part : (c + 1) * part, :] += dot(mixed[0], att, TN)

    @pl.when(step == pl.num_programs(0) - 1)
    def _():
        turned = jnp.broadcast_to(gain_sum[...], (LANES, features)).T
        lane = iota((features, LANES), 1)
        slot = iota((LANES, LANES), 0)
        slot = jnp.where(slot < experts, slot ^ order_ref[grad_w_ref.shape[0]], slot)
        swapped = jnp.where(slot == iota((LANES, LANES), 1), 1.0, 0.0).astype(BF16)
        side[...] = jnp.where(lane == experts, turned, dot(side[...].astype(BF16), swapped))
        block = grad_w_ref.shape[1]
        for k in range(grad_w_ref.shape[0]):
            start = pl.multiple_of(order_ref[k] * block, 32)
            grad_w_ref[k, :, :features] = total[pl.ds(start, block), :].astype(BF16)
            grad_w_ref[k, :, features:] = side[pl.ds(start, block), :].astype(BF16)


def back(places, experts, order, resid, logits, cot, mixed, summed, w, gain, router):
    images, tall, features = resid.shape
    shapes = [
        ((images, places, features), BF16),
        ((images, tall, features), BF16),
        ((images, tall, features), BF16),
    ]
    grad_w = (w.shape[0], w.shape[1], features + LANES)
    return pl.pallas_call(
        functools.partial(back_body, places, experts),
        grid=(images,),
        in_specs=[SMEM, spec_image(resid.shape), spec_image(logits.shape), spec_image(cot.shape)]
        + [spec_image(m.shape) for m in mixed]
        + [spec_image(summed.shape)]
        + [spec_whole(w.shape), spec_whole(gain.shape), spec_whole(router.shape)],
        out_specs=[spec_image(s) for s, _ in shapes] + [spec_whole(grad_w)],
        out_shape=[jax.ShapeDtypeStruct(s, t) for s, t in shapes]
        + [jax.ShapeDtypeStruct(grad_w, BF16)],
        scratch_shapes=[
            pltpu.VMEM((features, features), BF16),
            pltpu.VMEM((LANES, 2 * features), BF16),
            pltpu.VMEM((features, features), F32),
            pltpu.VMEM((features, LANES), F32),
            pltpu.VMEM((1, features), F32),
        ],
        compiler_params=params(),
        cost_estimate=cost(8 * images * tall * features * features, 16e6),
        name="back",
    )(order, resid, logits, cot, *mixed, summed, w, gain, router)


def attend_back_body(order_ref, joint_ref, prob_ref, grad_ref, mixed_ref, act_ref, out_ref, grad_w_ref, total):
    step = pl.program_id(0)

    @pl.when(step == 0)
    def _():
        total[...] = jnp.zeros_like(total)

    tall, width = joint_ref.shape[1:]
    third = width // 3
    low = iota((tall, LANES), 1) < LANES // 2
    for pair in range(third // LANES):
        query, keys, values = (
            joint_ref[0, :, part * third + pair * LANES : part * third + (pair + 1) * LANES]
            for part in range(3)
        )
        grad = grad_ref[0, :, pair * LANES : (pair + 1) * LANES]
        product = grad.astype(F32) * mixed_ref[0, :, pair * LANES : (pair + 1) * LANES].astype(F32)
        grads = []
        for side in range(2):
            mine = low if side == 0 else ~low
            prob = prob_ref[0, 2 * pair + side]
            inner = jnp.sum(jnp.where(mine, product, 0.0), axis=1, keepdims=True)
            grad_prob = dot(jnp.where(mine, grad, 0), values, NT)
            grad_scores = (prob.astype(F32) * (grad_prob - inner) * 0.125).astype(BF16)
            grads.append(
                (dot(grad_scores, keys), dot(grad_scores, query, TN), dot(prob, grad, TN))
            )
        for part in range(3):
            joined = jnp.where(low, grads[0][part], grads[1][part]).astype(BF16)
            out_ref[0, :, part * third + pair * LANES : part * third + (pair + 1) * LANES] = joined
    total[...] += dot(act_ref[0], out_ref[0], TN)

    @pl.when(step == pl.num_programs(0) - 1)
    def _():
        block = grad_w_ref.shape[1]
        for k in range(grad_w_ref.shape[0]):
            start = pl.multiple_of(order_ref[k] * block, 32)
            grad_w_ref[k] = total[pl.ds(start, block), :].astype(BF16)


def attend_back(blocks, chunk, order, joint, prob, grad_mixed, mixed, act):
    images, tall, width = joint.shape
    features = act.shape[-1]
    third = width // 3
    grad_w = (blocks, features // blocks, width)
    return pl.pallas_call(
        attend_back_body,
        grid=(images,),
        in_specs=[
            SMEM,
            spec_image(joint.shape),
            spec_image(prob.shape),
            pl.BlockSpec((1, tall, third), lambda i: (i, 0, chunk)),
            spec_image(mixed.shape),
            spec_image(act.shape),
        ],
        out_specs=[spec_image(joint.shape), spec_whole(grad_w)],
        out_shape=[
            jax.ShapeDtypeStruct(joint.shape, BF16),
            jax.ShapeDtypeStruct(grad_w, BF16),
        ],
        scratch_shapes=[pltpu.VMEM((features, width), F32)],
        compiler_params=params(),
        cost_estimate=cost(2 * images * tall * features * width * 5, 16e6),
        name="attend_back",
    )(order, joint, prob, grad_mixed, mixed, act)


def finish_body(places, order_ref, token_ref, att_ref, j0, j1, j2, w0, w1, w2, gain_ref, out_ref, s0, s1, s2):
    @pl.when(pl.program_id(0) == 0)
    def _():
        for source, target in ((w0, s0), (w1, s1), (w2, s2)):
            place_rows(order_ref, source, target)

    grad_act = dot(j0[0], s0[...], NT) + dot(j1[0], s1[...], NT) + dot(j2[0], s2[...], NT)
    normed, factor = normalize(token_ref[0].astype(F32))
    result = att_ref[0].astype(F32) + norm_back(grad_act, gain_ref[...], normed, factor)
    out_ref[0] = result[:places].astype(BF16)


def finish(places, order, tokens, att, joints, weights, gain):
    images, tall, features = tokens.shape
    shape = (images, places, features)
    return pl.pallas_call(
        functools.partial(finish_body, places),
        grid=(images,),
        in_specs=[SMEM, spec_image(tokens.shape), spec_image(att.shape)]
        + [spec_image(j.shape) for j in joints]
        + [spec_whole(w.shape) for w in weights]
        + [spec_whole(gain.shape)],
        out_specs=spec_image(shape),
        out_shape=jax.ShapeDtypeStruct(shape, BF16),
        scratch_shapes=[pltpu.VMEM((features, w.shape[-1]), BF16) for w in weights],
        compiler_params=params(),
        cost_estimate=cost(6 * images * tall * features * features, 12e6),
        name="finish",
    )(order, tokens, att, *joints, *weights, gain)


def per_device(
    tokens, cotangent, heads_in, heads_out, slot_router, first_gain, second_gain, expert_in, expert_out
):
    images, places, features = tokens.shape
    experts = slot_router.shape[1]
    group = lax.axis_size("grp")
    reps = lax.axis_size("rep")
    me = lax.axis_index("grp")
    own_rows = heads_in.shape[0]
    direct = own_rows % 32 == 0
    blocks = group if direct else 8
    order = jnp.arange(blocks, dtype=jnp.int32)
    if direct:
        order = order ^ me
    chip = me // 2
    order = jnp.concatenate([order, chip[None]])
    tall = -(-places // 16) * 16
    slot_rows = -(-experts // 16) * 16
    chunks = 3
    part = features // chunks

    def gathered(values):
        relative = gather_rows(values, group)
        if direct:
            return relative
        return flip_blocks(relative, me).reshape(blocks, features // blocks, -1)

    def scattered(placed):
        if not direct:
            placed = flip_blocks(placed.reshape(group, own_rows, -1), me)
        return sum_rep(scatter_sum(placed, group), reps)

    def in_order(relative):
        if direct:
            relative = flip_blocks(relative, me)
        return relative.reshape(features, -1)

    small = jnp.concatenate([slot_router, first_gain[:, None], second_gain[:, None]], axis=1)
    small = jnp.pad(small, ((0, 0), (0, LANES - small.shape[1])))
    columns = heads_in.reshape(own_rows, 3, chunks, part)
    pieces = [columns[:, :, c].reshape(own_rows, 3 * part) for c in range(chunks)]
    start = gathered(jnp.concatenate([pieces[0], small], axis=1))
    rest = gathered(jnp.concatenate(pieces[1:] + [heads_out], axis=1))
    wide = 3 * part
    weights = [start[..., :wide], rest[..., :wide], rest[..., wide : 2 * wide]]
    full_out = rest[..., 2 * wide :]
    small = in_order(start[..., wide:])
    gain_one = small[:, experts].astype(F32)[None]
    gain_two = small[:, experts + 1].astype(F32)[None]
    router = flip_blocks(small[:, :experts].T, chip).T
    router = jnp.pad(router, ((0, 0), (0, LANES - experts)))

    grow = ((0, 0), (0, tall - places), (0, 0))
    source = jnp.pad(tokens, grow)
    cot = jnp.pad(cotangent, grow)

    act, joint, prob, mixed = attend(True, places, order, source, gain_one, weights[0])
    joints, probs, mixes = [joint], [prob], [mixed]
    for c in range(1, chunks):
        joint, prob, mixed = attend(False, places, order, act, gain_one, weights[c])
        joints.append(joint)
        probs.append(prob)
        mixes.append(mixed)
    resid, logits, packed = route(
        places, experts, slot_rows, order, source, cot, mixes, full_out, gain_two, router
    )

    leaving = packed[:, :experts].transpose(1, 0, 2)
    arrived = jnp.stack(
        [leaving[0]] + [swap(leaving[k], "grp", group, 2 * k) for k in range(1, experts)]
    )
    arrived = jnp.stack([arrived, swap(arrived, "grp", group, 1)])
    received = arrived.reshape(2 * experts * images, 2 * features)
    piece_in, piece_out = expert_in[0], expert_out[0]
    result = expert(received, piece_in, piece_out).reshape(2, experts, images, 2 * features)
    both = add_low(result[0], swap(result[1], "grp", group, 1))
    summed = jnp.stack(
        [both[0]] + [swap(both[k], "grp", group, 2 * k) for k in range(1, experts)], axis=1
    )
    summed = jnp.pad(summed, ((0, 0), (0, slot_rows - experts), (0, 0)))

    every = jnp.concatenate(
        [received]
        + [
            lax.ppermute(received, "rep", [(i, (i + k) % reps) for i in range(reps)])
            for k in range(1, reps)
        ]
    )

    output, att, grad_mixed, grad_out = back(
        places, experts, order, resid, logits, cot, mixes, summed, full_out, gain_two, router
    )
    early = scattered(grad_out).astype(F32)
    grad_joints, shares = [], []
    for c in range(chunks):
        grad_joint, grad_w = attend_back(
            blocks, c, order, joints[c], probs[c], grad_mixed, mixes[c], act
        )
        grad_joints.append(grad_joint)
        shares.append(scattered(grad_w).astype(F32))
    expert_in_grad, expert_out_grad = expert_grad(every, piece_in, piece_out)
    token_grad = finish(places, order, source, att, grad_joints, weights, gain_one)

    late = jnp.stack([share.reshape(own_rows, 3, part) for share in shares], axis=2)
    late = late.reshape(own_rows, 3 * features)
    gain_one_grad = jnp.sum(late * heads_in.astype(F32), axis=1) / first_gain.astype(F32)
    return (
        output,
        token_grad,
        late,
        early[:, :features],
        early[:, features : features + experts],
        gain_one_grad,
        early[:, features + experts],
        expert_in_grad[None],
        expert_out_grad[None],
    )


def solution(mesh):
    token_spec = P(("rep", "grp"), None, None)
    matrix, vector, stack = P("grp", None), P("grp"), P("grp", None, None)
    return jax.shard_map(
        per_device,
        mesh=mesh,
        in_specs=(token_spec, token_spec, matrix, matrix, matrix, vector, vector, stack, stack),
        out_specs=(token_spec, token_spec, matrix, matrix, matrix, vector, vector, stack, stack),
        check_vma=False,
    )
```

profile of v0, /device:TPU:0, one launch (start us, length us, event | category | flops | bytes accessed | tf_op | source)
XLA Modules:
  0.0 252.1 jit_solution(1592121426633311185)
XLA Ops:
  5.2 3.0 %collective-permute-start.2 = (bf16[1,48,896]{2,1,0:T(8,128)(2,1)S(1)}, bf16[1,48,896]{2,1,0:T(8,128)(2,1)S(1)}, u32[]{:S(2)}, u32[]{:S(2)}) collective-permute-start(bf16[1,48,896]{2,1,0:T(8,128)(2,1)S(1)} %get-tuple-element.173), channel_id=1, source_target_pairs={{0,4},{1,5},{2,6},{3,7},{4,0},{5,1},{6,2},{7,3},{8,12},{9,13},{10,... | collective-permute-start | bytes 258056 | tf_op jit(solution)/shard_map/ppermute | solution.py:27
  19.2 2.9 %collective-permute-done.3 = bf16[2,48,896]{2,1,0:T(8,128)(2,1)S(1)} collective-permute-done((bf16[2,48,896]{2,1,0:T(8,128)(2,1)S(1)}, bf16[2,48,896]{2,1,0:T(8,128)(2,1)S(1)}, u32[]{:S(2)}, u32[]{:S(2)}) %collective-permute-start.3) | collective-permute-done | bytes 172064 | tf_op jit(solution)/shard_map/ppermute | solution.py:27
  24.4 6.2 %collective-permute-done.8 = bf16[2,48,2304]{2,1,0:T(8,128)(2,1)S(1)} collective-permute-done((bf16[2,48,2304]{2,1,0:T(8,128)(2,1)S(1)}, bf16[2,48,2304]{2,1,0:T(8,128)(2,1)S(1)}, u32[]{:S(2)}, u32[]{:S(2)}) %collective-permute-start.8) | collective-permute-done | bytes 442400 | tf_op jit(solution)/shard_map/ppermute | solution.py:27
  37.0 11.6 %attend.3 = (bf16[6,208,768]{2,1,0:T(8,128)(2,1)}, bf16[6,208,768]{2,1,0:T(8,128)(2,1)}, bf16[6,4,208,208]{3,2,1,0:T(8,128)(2,1)}, bf16[6,208,256]{2,1,0:T(8,128)(2,1)}) custom-call(s32[9]{0:T(128)} %pad_add_fusion.order_ref, bf16[6,208,768]{2,1,0:T(8,128)(2,1)} %pad.19.source_ref.token_ref, f32[1,768]{1,0:T(1,128)} %bitcast_convert_fusion.1.gain_ref, ...), custom_call_target="tpu_custom_call" | custom-call | flops 4416602112 | bytes 8000000 | tf_op jit(solution)/shard_map/attend/pallas_call | solution.py:199
  52.5 10.4 %attend.4 = (bf16[6,208,768]{2,1,0:T(8,128)(2,1)}, bf16[6,4,208,208]{3,2,1,0:T(8,128)(2,1)}, bf16[6,208,256]{2,1,0:T(8,128)(2,1)}) custom-call(s32[9]{0:T(128)} %pad_add_fusion.order_ref, bf16[6,208,768]{2,1,0:T(8,128)(2,1)} %get-tuple-element.35.source_ref.act_ref, f32[1,768]{1,0:T(1,128)} %bitcast_convert_fusion.1.gain_ref, ...), custom_call_target="tpu_custom_call" | custom-call | flops 4416602112 | bytes 8000000 | tf_op jit(solution)/shard_map/attend/pallas_call | solution.py:199
  62.9 10.4 %attend.5 = (bf16[6,208,768]{2,1,0:T(8,128)(2,1)}, bf16[6,4,208,208]{3,2,1,0:T(8,128)(2,1)}, bf16[6,208,256]{2,1,0:T(8,128)(2,1)}) custom-call(s32[9]{0:T(128)} %pad_add_fusion.order_ref, bf16[6,208,768]{2,1,0:T(8,128)(2,1)} %get-tuple-element.35.source_ref.act_ref, f32[1,768]{1,0:T(1,128)} %bitcast_convert_fusion.1.gain_ref, ...), custom_call_target="tpu_custom_call" | custom-call | flops 4416602112 | bytes 8000000 | tf_op jit(solution)/shard_map/attend/pallas_call | solution.py:199
  73.3 10.8 %route.1 = (f32[6,208,768]{2,1,0:T(8,128)}, f32[6,208,128]{2,1,0:T(8,128)}, bf16[6,16,1536]{2,1,0:T(8,128)(2,1)}) custom-call(s32[9]{0:T(128)} %pad_add_fusion.order_ref, bf16[6,208,768]{2,1,0:T(8,128)(2,1)} %pad.19.source_ref.token_ref, bf16[6,208,768]{2,1,0:T(8,128)(2,1)} %pad.20.cot_ref, bf16[6,208,256]{2,1,0:T(8,128)(2,1)} %get-tuple-element.34.m0.mixed_ref, ...), custom_call_target="tpu_custom_call" | custom-call | flops 2944401408 | bytes 8000000 | tf_op jit(solution)/shard_map/route/pallas_call | solution.py:255
  93.8 5.4 %expert.1 = bf16[48,1536]{1,0:T(8,128)(2,1)} custom-call(bf16[48,1536]{1,0:T(8,128)(2,1)} %reshape.236.rows_ref, bf16[768,1536]{1,0:T(8,128)(2,1)} %bitcast.287, bf16[1536,768]{1,0:T(8,128)(2,1)} %bitcast.289), custom_call_target="tpu_custom_call" | custom-call | flops 2415919104 | bytes 5000000 | tf_op jit(solution)/shard_map/expert/pallas_call | solution.py:297
  101.5 2.2 collective-permute-start.17
  105.1 4.0 %collective-permute-start.48 = (bf16[48,1536]{1,0:T(8,128)(2,1)S(1)}, bf16[48,1536]{1,0:T(8,128)(2,1)S(1)}, u32[]{:S(2)}, u32[]{:S(2)}) collective-permute-start(bf16[48,1536]{1,0:T(8,128)(2,1)S(1)} %copy-done.8), channel_id=1, source_target_pairs={{0,24},{8,0},{16,8},{24,16},{1,25},{9,1},{17,9},{25,17},{2,26},{10... | collective-permute-start | bytes 442376 | tf_op jit(solution)/shard_map/ppermute | solution.py:611
  111.3 16.7 %back.1 = (bf16[6,197,768]{2,1,0:T(8,128)(2,1)}, bf16[6,208,768]{2,1,0:T(8,128)(2,1)}, bf16[6,208,768]{2,1,0:T(8,128)(2,1)}, bf16[8,96,896]{2,1,0:T(8,128)(2,1)}) custom-call(s32[9]{0:T(128)} %pad_add_fusion.order_ref, f32[6,208,768]{2,1,0:T(8,128)} %get-tuple-element.38.resid_ref, f32[6,208,128]{2,1,0:T(8,128)} %get-tuple-element.39.logit_ref, ...), custom_call_target="tpu_custom_call" | custom-call | flops 5888802816 | bytes 16000000 | tf_op jit(solution)/shard_map/back/pallas_call | solution.py:405
  128.0 13.3 %attend_back.5 = (bf16[6,208,768]{2,1,0:T(8,128)(2,1)}, bf16[8,96,768]{2,1,0:T(8,128)(2,1)}) custom-call(s32[9]{0:T(128)} %pad_add_fusion.order_ref, bf16[6,208,768]{2,1,0:T(8,128)(2,1)} %get-tuple-element.50.joint_ref, bf16[6,4,208,208]{3,2,1,0:T(8,128)(2,1)} %get-tuple-element.51.prob_ref, bf16[6,208,768]{2,1,0:T(8,128)(2,1)} %get-tuple-element.45.grad_ref, ...), custom_call_target="tpu_custom_call" | custom-call | flops 7361003520 | bytes 16000000 | tf_op jit(solution)/shard_map/attend_back/pallas_call | solution.py:473
  142.6 13.2 %attend_back.4 = (bf16[6,208,768]{2,1,0:T(8,128)(2,1)}, bf16[8,96,768]{2,1,0:T(8,128)(2,1)}) custom-call(s32[9]{0:T(128)} %pad_add_fusion.order_ref, bf16[6,208,768]{2,1,0:T(8,128)(2,1)} %get-tuple-element.47.joint_ref, bf16[6,4,208,208]{3,2,1,0:T(8,128)(2,1)} %get-tuple-element.48.prob_ref, bf16[6,208,768]{2,1,0:T(8,128)(2,1)} %get-tuple-element.45.grad_ref, ...), custom_call_target="tpu_custom_call" | custom-call | flops 7361003520 | bytes 16000000 | tf_op jit(solution)/shard_map/attend_back/pallas_call | solution.py:473
  157.6 13.3 %attend_back.3 = (bf16[6,208,768]{2,1,0:T(8,128)(2,1)}, bf16[8,96,768]{2,1,0:T(8,128)(2,1)}) custom-call(s32[9]{0:T(128)} %pad_add_fusion.order_ref, bf16[6,208,768]{2,1,0:T(8,128)(2,1)} %get-tuple-element.43.joint_ref, bf16[6,4,208,208]{3,2,1,0:T(8,128)(2,1)} %get-tuple-element.44.prob_ref, bf16[6,208,768]{2,1,0:T(8,128)(2,1)} %get-tuple-element.45.grad_ref, ...), custom_call_target="tpu_custom_call" | custom-call | flops 7361003520 | bytes 16000000 | tf_op jit(solution)/shard_map/attend_back/pallas_call | solution.py:473
  172.2 12.9 %finish.1 = bf16[6,197,768]{2,1,0:T(8,128)(2,1)} custom-call(s32[9]{0:T(128)} %pad_add_fusion.order_ref, bf16[6,208,768]{2,1,0:T(8,128)(2,1)} %pad.19.source_ref.token_ref, bf16[6,208,768]{2,1,0:T(8,128)(2,1)} %get-tuple-element.42.att_ref, bf16[6,208,768]{2,1,0:T(8,128)(2,1)} %get-tuple-element.46.j0, bf16[6,208,768]{2,1,0:T(8,128)(2,1)} %get-tuple-element.49.j1, ...), custom_call_target="tpu_custom_call" | custom-call | flops 4416602112 | bytes 12000000 | tf_op jit(solution)/shard_map/finish/pallas_call | solution.py:511
  186.8 8.1 %expert_grad.1 = (f32[768,1536]{1,0:T(8,128)}, f32[1536,768]{1,0:T(8,128)}) custom-call(bf16[192,1536]{1,0:T(8,128)(2,1)} %pad_maximum_fusion.6.rows_ref, bf16[768,1536]{1,0:T(8,128)(2,1)} %bitcast.288, bf16[1536,768]{1,0:T(8,128)(2,1)} %bitcast.290), custom_call_target="tpu_custom_call" | custom-call | flops 1811939328 | bytes 14000000 | tf_op jit(solution)/shard_map/expert_grad/pallas_call | solution.py:323
  210.7 3.9 %collective-permute-done.34 = bf16[1,96,384]{2,1,0:T(8,128)(2,1)S(1)} collective-permute-done((bf16[1,96,384]{2,1,0:T(8,128)(2,1)S(1)}, bf16[1,96,384]{2,1,0:T(8,128)(2,1)S(1)}, u32[]{:S(2)}, u32[]{:S(2)}) %collective-permute-start.34) | collective-permute-done | bytes 73760 | tf_op jit(solution)/shard_map/ppermute | solution.py:27
  218.9 2.5 collective-permute-start.37
  225.9 2.2 collective-permute-done.41
  229.8 2.5 collective-permute-start.31
  233.9 3.0 %collective-permute-done.38 = bf16[96,768]{1,0:T(8,128)(2,1)S(1)} collective-permute-done((bf16[96,768]{1,0:T(8,128)(2,1)S(1)}, bf16[96,768]{1,0:T(8,128)(2,1)S(1)}, u32[]{:S(2)}, u32[]{:S(2)}) %collective-permute-start.38) | collective-permute-done | bytes 147488 | tf_op jit(solution)/shard_map/ppermute | solution.py:27
  237.0 2.2 collective-permute-done.31
  242.6 2.9 %collective-permute-start.45 = (bf16[96,896]{1,0:T(8,128)(2,1)S(1)}, bf16[96,896]{1,0:T(8,128)(2,1)S(1)}, u32[]{:S(2)}, u32[]{:S(2)}) collective-permute-start(bf16[96,896]{1,0:T(8,128)(2,1)S(1)} %add_convert_fusion.1), channel_id=1, source_target_pairs={{0,24},{8,16},{16,8},{24,0},{1,25},{9,17},{17,9},{25,1},{2,26},{10... | collective-permute-start | bytes 516104 | tf_op jit(solution)/shard_map/ppermute | solution.py:27
  246.0 4.0 %collective-permute-done.45 = bf16[96,896]{1,0:T(8,128)(2,1)S(1)} collective-permute-done((bf16[96,896]{1,0:T(8,128)(2,1)S(1)}, bf16[96,896]{1,0:T(8,128)(2,1)S(1)}, u32[]{:S(2)}, u32[]{:S(2)}) %collective-permute-start.45) | collective-permute-done | bytes 172064 | tf_op jit(solution)/shard_map/ppermute | solution.py:27
  (255 shorter events, 82.8 us)
Async XLA Ops:
  5.2 9.5 %collective-permute-start.2 = (bf16[1,48,896]{2,1,0:T(8,128)(2,1)S(1)}, bf16[1,48,896]{2,1,0:T(8,128)(2,1)S(1)}, u32[]{:S(2)}, u32[]{:S(2)}) collective-permute-start(bf16[1,48,896]{2,1,0:T(8,128)(2,1)S(1)} %get-tuple-element.173), channel_id=1, source_target_pairs={{0,4},{1,5},{2,6},{3,7},{4,0},{5,1},{6,2},{7,3},{8,12},{9,13},{10,... | collective-permute-start | bytes 258056 | tf_op jit(solution)/shard_map/ppermute | solution.py:27
  8.3 8.5 %collective-permute-start = (bf16[1,48,896]{2,1,0:T(8,128)(2,1)S(1)}, bf16[1,48,896]{2,1,0:T(8,128)(2,1)S(1)}, u32[]{:S(2)}, u32[]{:S(2)}) collective-permute-start(bf16[1,48,896]{2,1,0:T(8,128)(2,1)S(1)} %get-tuple-element.172), channel_id=1, source_target_pairs={{0,2},{1,3},{2,0},{3,1},{4,6},{5,7},{6,4},{7,5},{8,10},{9,11},{10,... | collective-permute-start | bytes 258056 | tf_op jit(solution)/shard_map/ppermute | solution.py:27
  9.9 8.5 %collective-permute-start.7 = (bf16[1,48,2304]{2,1,0:T(8,128)(2,1)S(1)}, bf16[1,48,2304]{2,1,0:T(8,128)(2,1)S(1)}, u32[]{:S(2)}, u32[]{:S(2)}) collective-permute-start(bf16[1,48,2304]{2,1,0:T(8,128)(2,1)S(1)} %get-tuple-element.161), channel_id=1, source_target_pairs={{0,4},{1,5},{2,6},{3,7},{4,0},{5,1},{6,2},{7,3},{8,12},{9,13},{10,... | collective-permute-start | bytes 663560 | tf_op jit(solution)/shard_map/ppermute | solution.py:27
  10.5 8.6 %collective-permute-start.5 = (bf16[1,48,2304]{2,1,0:T(8,128)(2,1)S(1)}, bf16[1,48,2304]{2,1,0:T(8,128)(2,1)S(1)}, u32[]{:S(2)}, u32[]{:S(2)}) collective-permute-start(bf16[1,48,2304]{2,1,0:T(8,128)(2,1)S(1)} %get-tuple-element.160), channel_id=1, source_target_pairs={{0,2},{1,3},{2,0},{3,1},{4,6},{5,7},{6,4},{7,5},{8,10},{9,11},{10,... | collective-permute-start | bytes 663560 | tf_op jit(solution)/shard_map/ppermute | solution.py:27
  18.5 12.2 %collective-permute-start.8 = (bf16[2,48,2304]{2,1,0:T(8,128)(2,1)S(1)}, bf16[2,48,2304]{2,1,0:T(8,128)(2,1)S(1)}, u32[]{:S(2)}, u32[]{:S(2)}) collective-permute-start(bf16[2,48,2304]{2,1,0:T(8,128)(2,1)S(1)} %pad_maximum_fusion.8), channel_id=1, source_target_pairs={{0,2},{1,3},{2,0},{3,1},{4,6},{5,7},{6,4},{7,5},{8,10},{9,11},{10,... | collective-permute-start | bytes 1327112 | tf_op jit(solution)/shard_map/ppermute | solution.py:27
  19.1 12.0 %collective-permute-start.6 = (bf16[2,48,2304]{2,1,0:T(8,128)(2,1)S(1)}, bf16[2,48,2304]{2,1,0:T(8,128)(2,1)S(1)}, u32[]{:S(2)}, u32[]{:S(2)}) collective-permute-start(bf16[2,48,2304]{2,1,0:T(8,128)(2,1)S(1)} %pad_maximum_fusion.7), channel_id=1, source_target_pairs={{0,4},{1,5},{2,6},{3,7},{4,0},{5,1},{6,2},{7,3},{8,12},{9,13},{10,... | collective-permute-start | bytes 1327112 | tf_op jit(solution)/shard_map/ppermute | solution.py:27
  32.4 16.2 %collective-permute-start.9 = (bf16[4,96,2304]{2,1,0:T(8,128)(2,1)}, bf16[4,96,2304]{2,1,0:T(8,128)(2,1)}, u32[]{:S(2)}, u32[]{:S(2)}) collective-permute-start(bf16[4,96,2304]{2,1,0:T(8,128)(2,1)} %maximum_maximum_fusion), channel_id=1, source_target_pairs={{0,1},{1,0},{2,3},{3,2},{4,5},{5,4},{6,7},{7,6},{8,9},{9,8},{10,11... | collective-permute-start | bytes 5308424 | tf_op jit(solution)/shard_map/ppermute | solution.py:27
  105.1 80.2 %collective-permute-start.48 = (bf16[48,1536]{1,0:T(8,128)(2,1)S(1)}, bf16[48,1536]{1,0:T(8,128)(2,1)S(1)}, u32[]{:S(2)}, u32[]{:S(2)}) collective-permute-start(bf16[48,1536]{1,0:T(8,128)(2,1)S(1)} %copy-done.8), channel_id=1, source_target_pairs={{0,24},{8,0},{16,8},{24,16},{1,25},{9,1},{17,9},{25,17},{2,26},{10... | collective-permute-start | bytes 442376 | tf_op jit(solution)/shard_map/ppermute | solution.py:611
  109.1 76.3 %collective-permute-start.47 = (bf16[48,1536]{1,0:T(8,128)(2,1)S(1)}, bf16[48,1536]{1,0:T(8,128)(2,1)S(1)}, u32[]{:S(2)}, u32[]{:S(2)}) collective-permute-start(bf16[48,1536]{1,0:T(8,128)(2,1)S(1)} %copy-done.8), channel_id=1, source_target_pairs={{0,16},{8,24},{16,0},{24,8},{1,17},{9,25},{17,1},{25,9},{2,18},{10... | collective-permute-start | bytes 442376 | tf_op jit(solution)/shard_map/ppermute | solution.py:611
  109.2 76.7 %collective-permute-start.46 = (bf16[48,1536]{1,0:T(8,128)(2,1)S(1)}, bf16[48,1536]{1,0:T(8,128)(2,1)S(1)}, u32[]{:S(2)}, u32[]{:S(2)}) collective-permute-start(bf16[48,1536]{1,0:T(8,128)(2,1)S(1)} %copy-done.8), channel_id=1, source_target_pairs={{0,8},{8,16},{16,24},{24,0},{1,9},{9,17},{17,25},{25,1},{2,10},{10... | collective-permute-start | bytes 442376 | tf_op jit(solution)/shard_map/ppermute | solution.py:611
  142.5 52.3 %collective-permute-start.32 = (bf16[4,96,768]{2,1,0:T(8,128)(2,1)S(1)}, bf16[4,96,768]{2,1,0:T(8,128)(2,1)S(1)}, u32[]{:S(2)}, u32[]{:S(2)}) collective-permute-start(bf16[4,96,768]{2,1,0:T(8,128)(2,1)S(1)} %pad_maximum_fusion.5), channel_id=1, source_target_pairs={{0,1},{1,0},{2,3},{3,2},{4,5},{5,4},{6,7},{7,6},{8,9},{9,8},{10,11... | collective-permute-start | bytes 1769480 | tf_op jit(solution)/shard_map/ppermute | solution.py:27
  157.1 40.5 %collective-permute-start.25 = (bf16[4,96,768]{2,1,0:T(8,128)(2,1)S(1)}, bf16[4,96,768]{2,1,0:T(8,128)(2,1)S(1)}, u32[]{:S(2)}, u32[]{:S(2)}) collective-permute-start(bf16[4,96,768]{2,1,0:T(8,128)(2,1)S(1)} %pad_maximum_fusion.4), channel_id=1, source_target_pairs={{0,1},{1,0},{2,3},{3,2},{4,5},{5,4},{6,7},{7,6},{8,9},{9,8},{10,11... | collective-permute-start | bytes 1769480 | tf_op jit(solution)/shard_map/ppermute | solution.py:27
  185.3 13.1 %collective-permute-start.18 = (bf16[4,96,768]{2,1,0:T(8,128)(2,1)S(1)}, bf16[4,96,768]{2,1,0:T(8,128)(2,1)S(1)}, u32[]{:S(2)}, u32[]{:S(2)}) collective-permute-start(bf16[4,96,768]{2,1,0:T(8,128)(2,1)S(1)} %pad_maximum_fusion.3), channel_id=1, source_target_pairs={{0,1},{1,0},{2,3},{3,2},{4,5},{5,4},{6,7},{7,6},{8,9},{9,8},{10,11... | collective-permute-start | bytes 1769480 | tf_op jit(solution)/shard_map/ppermute | solution.py:27
  185.4 14.5 %collective-permute-start.39 = (bf16[4,96,896]{2,1,0:T(8,128)(2,1)S(1)}, bf16[4,96,896]{2,1,0:T(8,128)(2,1)S(1)}, u32[]{:S(2)}, u32[]{:S(2)}) collective-permute-start(bf16[4,96,896]{2,1,0:T(8,128)(2,1)S(1)} %pad_maximum_fusion.2), channel_id=1, source_target_pairs={{0,1},{1,0},{2,3},{3,2},{4,5},{5,4},{6,7},{7,6},{8,9},{9,8},{10,11... | collective-permute-start | bytes 2064392 | tf_op jit(solution)/shard_map/ppermute | solution.py:27
  202.8 22.5 %collective-permute-start.42 = (bf16[2,96,512]{2,1,0:T(8,128)(2,1)S(1)}, bf16[2,96,512]{2,1,0:T(8,128)(2,1)S(1)}, u32[]{:S(2)}, u32[]{:S(2)}) collective-permute-start(bf16[2,96,512]{2,1,0:T(8,128)(2,1)S(1)} %pad_maximum_fusion.11), channel_id=1, source_target_pairs={{0,4},{1,5},{2,6},{3,7},{4,0},{5,1},{6,2},{7,3},{8,12},{9,13},{10,... | collective-permute-start | bytes 589832 | tf_op jit(solution)/shard_map/ppermute | solution.py:27
  205.0 18.7 %collective-permute-start.40 = (bf16[2,96,384]{2,1,0:T(8,128)(2,1)S(1)}, bf16[2,96,384]{2,1,0:T(8,128)(2,1)S(1)}, u32[]{:S(2)}, u32[]{:S(2)}) collective-permute-start(bf16[2,96,384]{2,1,0:T(8,128)(2,1)S(1)} %pad_maximum_fusion.25), channel_id=1, source_target_pairs={{0,2},{1,3},{2,0},{3,1},{4,6},{5,7},{6,4},{7,5},{8,10},{9,11},{10,... | collective-permute-start | bytes 442376 | tf_op jit(solution)/shard_map/ppermute | solution.py:27
  206.0 8.6 %collective-permute-start.34 = (bf16[1,96,384]{2,1,0:T(8,128)(2,1)S(1)}, bf16[1,96,384]{2,1,0:T(8,128)(2,1)S(1)}, u32[]{:S(2)}, u32[]{:S(2)}) collective-permute-start(bf16[1,96,384]{2,1,0:T(8,128)(2,1)S(1)} %fusion.56), channel_id=1, source_target_pairs={{0,4},{1,5},{2,6},{3,7},{4,0},{5,1},{6,2},{7,3},{8,12},{9,13},{10,... | collective-permute-start | bytes 221192 | tf_op jit(solution)/shard_map/ppermute | solution.py:27
  218.9 9.3 %collective-permute-start.37 = (bf16[96,768]{1,0:T(8,128)(2,1)S(1)}, bf16[96,768]{1,0:T(8,128)(2,1)S(1)}, u32[]{:S(2)}, u32[]{:S(2)}) collective-permute-start(bf16[96,768]{1,0:T(8,128)(2,1)S(1)} %pad_maximum_fusion.24), channel_id=1, source_target_pairs={{0,8},{8,0},{16,24},{24,16},{1,9},{9,1},{17,25},{25,17},{2,10},{10... | collective-permute-start | bytes 442376 | tf_op jit(solution)/shard_map/ppermute | solution.py:27
  222.7 9.6 %collective-permute-start.23 = (bf16[96,768]{1,0:T(8,128)(2,1)S(1)}, bf16[96,768]{1,0:T(8,128)(2,1)S(1)}, u32[]{:S(2)}, u32[]{:S(2)}) collective-permute-start(bf16[96,768]{1,0:T(8,128)(2,1)S(1)} %pad_maximum_fusion.18), channel_id=1, source_target_pairs={{0,8},{8,0},{16,24},{24,16},{1,9},{9,1},{17,25},{25,17},{2,10},{10... | collective-permute-start | bytes 442376 | tf_op jit(solution)/shard_map/ppermute | solution.py:27
  225.3 8.4 %collective-permute-start.43 = (bf16[1,96,512]{2,1,0:T(8,128)(2,1)S(1)}, bf16[1,96,512]{2,1,0:T(8,128)(2,1)S(1)}, u32[]{:S(2)}, u32[]{:S(2)}) collective-permute-start(bf16[1,96,512]{2,1,0:T(8,128)(2,1)S(1)} %fusion.50), channel_id=1, source_target_pairs={{0,2},{1,3},{2,0},{3,1},{4,6},{5,7},{6,4},{7,5},{8,10},{9,11},{10,... | collective-permute-start | bytes 294920 | tf_op jit(solution)/shard_map/ppermute | solution.py:27
  228.3 8.6 %collective-permute-start.38 = (bf16[96,768]{1,0:T(8,128)(2,1)S(1)}, bf16[96,768]{1,0:T(8,128)(2,1)S(1)}, u32[]{:S(2)}, u32[]{:S(2)}) collective-permute-start(bf16[96,768]{1,0:T(8,128)(2,1)S(1)} %add_convert_fusion.7), channel_id=1, source_target_pairs={{0,24},{8,16},{16,8},{24,0},{1,25},{9,17},{17,9},{25,1},{2,26},{10... | collective-permute-start | bytes 442376 | tf_op jit(solution)/shard_map/ppermute | solution.py:27
  229.8 9.5 %collective-permute-start.31 = (bf16[96,768]{1,0:T(8,128)(2,1)S(1)}, bf16[96,768]{1,0:T(8,128)(2,1)S(1)}, u32[]{:S(2)}, u32[]{:S(2)}) collective-permute-start(bf16[96,768]{1,0:T(8,128)(2,1)S(1)} %add_convert_fusion.13), channel_id=1, source_target_pairs={{0,24},{8,16},{16,8},{24,0},{1,25},{9,17},{17,9},{25,1},{2,26},{10... | collective-permute-start | bytes 442376 | tf_op jit(solution)/shard_map/ppermute | solution.py:27
  232.3 8.5 %collective-permute-start.24 = (bf16[96,768]{1,0:T(8,128)(2,1)S(1)}, bf16[96,768]{1,0:T(8,128)(2,1)S(1)}, u32[]{:S(2)}, u32[]{:S(2)}) collective-permute-start(bf16[96,768]{1,0:T(8,128)(2,1)S(1)} %add_convert_fusion.19), channel_id=1, source_target_pairs={{0,24},{8,16},{16,8},{24,0},{1,25},{9,17},{17,9},{25,1},{2,26},{10... | collective-permute-start | bytes 442376 | tf_op jit(solution)/shard_map/ppermute | solution.py:27
  233.8 8.7 %collective-permute-start.44 = (bf16[96,896]{1,0:T(8,128)(2,1)S(1)}, bf16[96,896]{1,0:T(8,128)(2,1)S(1)}, u32[]{:S(2)}, u32[]{:S(2)}) collective-permute-start(bf16[96,896]{1,0:T(8,128)(2,1)S(1)} %pad_maximum_fusion.14), channel_id=1, source_target_pairs={{0,8},{8,0},{16,24},{24,16},{1,9},{9,1},{17,25},{25,17},{2,10},{10... | collective-permute-start | bytes 516104 | tf_op jit(solution)/shard_map/ppermute | solution.py:27
  (36 other events, 224.0 us)
where the time goes:
time: 255 us; the launch traced here: 252 us
  Pallas kernels  126 us (49%)
  starting transfers between devices  54.3 us (21%)
  waiting for transfers between devices  36.1 us (14%)
  local copies, waits for them, and re-layouts  21.8 us (9%)
  other arithmetic  12.3 us (5%)
    ppermute x46, starting transfers between devices, swap(): lax.ppermute(values, axis, [(place, place ^ bit) for place in range(size)])  49.2 us
    pallas_call x3, Pallas kernels, attend_back(): pl.pallas_call(attend_back_body, grid=(images,), in_specs=[SMEM, spec_ima...  39.8 us
    ppermute x46, waiting for transfers between devices, swap(): lax.ppermute(values, axis, [(place, place ^ bit) for place in range(size)])  36.1 us
    pallas_call x3, Pallas kernels, attend(): pl.pallas_call(functools.partial(attend_body, first, places), grid=(image...  32.4 us
    pallas_call x1, Pallas kernels, back(): pl.pallas_call(functools.partial(back_body, places, experts), grid=(image...  16.7 us
    pallas_call x1, Pallas kernels, finish(): pl.pallas_call(functools.partial(finish_body, places), grid=(images,), in...  12.9 us
    pallas_call x1, Pallas kernels, route(): pl.pallas_call(functools.partial(route_body, places, experts), grid=(imag...  10.8 us
    pallas_call x1, Pallas kernels, expert_grad(): pl.pallas_call(expert_grad_body, grid=(hidden // step,), in_specs=[spec_w...  8.07 us
  transfers between devices with their start and end apart: 49, of which 23 were waited for; matrix products, arithmetic and copies ran while one was open for 8% of the time, Pallas kernels for 35%

commit v1 on v0

v1 whole, which is shorter than its diff:
```python
import functools

import jax
import jax.numpy as jnp
from jax import lax
from jax.experimental import pallas as pl
from jax.experimental.pallas import tpu as pltpu
from jax.sharding import PartitionSpec as P

HEADS = 12
LANES = 128
F32 = jnp.float32
BF16 = jnp.bfloat16
LOW = -1e30
VMEM_BYTES = 56 * 1024 * 1024

NN = (((1,), (0,)), ((), ()))
NT = (((1,), (1,)), ((), ()))
TN = (((0,), (0,)), ((), ()))


def dot(left, right, form=NN):
    return lax.dot_general(left, right, form, preferred_element_type=F32)


def swap(values, axis, size, bit):
    return lax.ppermute(values, axis, [(place, place ^ bit) for place in range(size)])


def bits_of(size):
    bit, bits = 1, []
    while bit < size:
        bits.append(bit)
        bit *= 2
    return bits


def flip_blocks(blocks, place):
    size = blocks.shape[0]
    for bit in bits_of(size):
        pairs = blocks.reshape((size // (2 * bit), 2, bit) + blocks.shape[1:])
        odd = (place & bit) > 0
        low, high = pairs[:, 0], pairs[:, 1]
        pairs = jnp.stack([jnp.where(odd, high, low), jnp.where(odd, low, high)], axis=1)
        blocks = pairs.reshape(blocks.shape)
    return blocks


def after(values, *others):
    return lax.optimization_barrier((values, others))[0]


def gather_stage(held, size, bit):
    return jnp.concatenate([held, swap(held, "grp", size, bit)])


def join_halves(first, second):
    second = jnp.stack([second[0], second[2], second[1], second[3]])
    return jnp.concatenate([first, second], axis=1)


def add_low(*terms):
    return sum(term.astype(F32) for term in terms).astype(BF16)


def spread_sum(keep, give):
    got = swap(give, "grp", 8, 1)
    sums = [add_low(keep[k], got[k]) for k in range(4)]
    return sums[0], [swap(sums[k], "grp", 8, 2 * k) for k in range(1, 4)], sums


def iota(shape, axis):
    return lax.broadcasted_iota(jnp.int32, shape, axis)


def normalize(values):
    center = values - jnp.mean(values, axis=-1, keepdims=True)
    factor = lax.rsqrt(jnp.mean(center * center, axis=-1, keepdims=True) + 1e-06)
    return center * factor, factor


def norm_back(scaled, normed, factor):
    inner = (
        scaled
        - jnp.mean(scaled, axis=-1, keepdims=True)
        - normed * jnp.mean(scaled * normed, axis=-1, keepdims=True)
    )
    return factor * inner


def place_rows(order_ref, source_ref, target_ref):
    blocks = source_ref.shape[0]
    rows = target_ref.shape[0] // blocks
    for k in range(blocks):
        start = pl.multiple_of(order_ref[k] * rows, 32)
        target_ref[pl.ds(start, rows), :] = source_ref[k, :rows]


def store_blocks(order_ref, source, keep_ref, give_ref, columns):
    half, rows = keep_ref.shape[:2]
    for k in range(2 * half):
        start = pl.multiple_of(order_ref[2 * half + k] * rows, 32)
        target = keep_ref if k < half else give_ref
        target[k % half, :, columns] = source[pl.ds(start, rows), :].astype(BF16)


def gather_small(order_ref, w_ref, rows, small_ref):
    blocks, high, _ = w_ref.shape
    block = small_ref.shape[1] // blocks
    total = jnp.zeros(small_ref.shape, F32)
    lane = iota((LANES, small_ref.shape[1]), 0)
    place = iota((LANES, small_ref.shape[1]), 1)
    for k in range(blocks):
        fits = (place == order_ref[k] * block + lane) & (lane < block)
        total = total + dot(w_ref[k, rows:high, :LANES], jnp.where(fits, 1.0, 0.0).astype(BF16))
    small_ref[...] = total


def attend_body(first, places, order_ref, source_ref, w_ref, *refs):
    if first:
        act_ref, small_ref, joint_ref, prob_ref, mixed_ref, weight = refs
    else:
        joint_ref, prob_ref, mixed_ref, weight = refs

    @pl.when(pl.program_id(0) == 0)
    def _():
        place_rows(order_ref, w_ref, weight)
        if first:
            gather_small(order_ref, w_ref, weight.shape[0] // w_ref.shape[0], small_ref)

    if first:
        normed, _ = normalize(source_ref[0].astype(F32))
        act = (normed * small_ref[0:1, :]).astype(BF16)
        act_ref[0] = act
    else:
        act = source_ref[0]
    joint = dot(act, weight[...]).astype(BF16)
    joint_ref[0] = joint
    tall = act.shape[0]
    third = joint.shape[1] // 3
    low = iota((tall, LANES), 1) < LANES // 2
    inside = iota((tall, LANES), 0) < places
    seen = iota((tall, tall), 1) < places
    for pair in range(third // LANES):
        query, keys, values = (
            joint[:, part * third + pair * LANES : part * third + (pair + 1) * LANES]
            for part in range(3)
        )
        query = query * 0.125
        outs = []
        for side in range(2):
            mine = low if side == 0 else ~low
            scores = dot(jnp.where(mine, query, 0), keys, NT)
            scores = jnp.where(seen, scores, LOW)
            power = jnp.exp(scores - jnp.max(scores, axis=1, keepdims=True))
            prob = (power * (1.0 / jnp.sum(power, axis=1, keepdims=True))).astype(BF16)
            prob_ref[0, 2 * pair + side] = prob
            outs.append(dot(prob, values))
        mixed = jnp.where(inside, jnp.where(low, outs[0], outs[1]), 0.0)
        mixed_ref[0, :, pair * LANES : (pair + 1) * LANES] = mixed.astype(BF16)


def spec_image(shape):
    count = len(shape)
    return pl.BlockSpec((1,) + shape[1:], lambda i: (i,) + (0,) * (count - 1))


def spec_whole(shape):
    count = len(shape)
    return pl.BlockSpec(shape, lambda i: (0,) * count)


SMEM = pl.BlockSpec(memory_space=pltpu.SMEM)


def params():
    return pltpu.CompilerParams(vmem_limit_bytes=VMEM_BYTES)


def cost(flops, data):
    return pl.CostEstimate(flops=int(flops), bytes_accessed=int(data), transcendentals=0)


def attend(first, places, order, source, w, columns):
    images, tall, features = source.shape
    width, start = columns
    heads = width // 3 // 64
    shapes = [
        ((images, tall, width), BF16),
        ((images, heads, tall, tall), BF16),
        ((images, tall, width // 3), BF16),
    ]
    specs = [spec_image(s) for s, _ in shapes]
    if first:
        small = (w.shape[1] - features // w.shape[0], features)
        specs = [spec_image(source.shape), spec_whole(small)] + specs
        shapes = [((images, tall, features), BF16), (small, F32)] + shapes
    return pl.pallas_call(
        functools.partial(attend_body, first, places),
        grid=(images,),
        in_specs=[
            SMEM,
            spec_image(source.shape),
            pl.BlockSpec(w.shape[:2] + (width,), lambda i: (0, 0, start)),
        ],
        out_specs=specs,
        out_shape=[jax.ShapeDtypeStruct(s, t) for s, t in shapes],
        scratch_shapes=[pltpu.VMEM((features, width), BF16)],
        compiler_params=params(),
        cost_estimate=cost(2 * images * tall * features * width * 3, 8e6),
        name="attend",
    )(order, source, w)


def spread_router(experts, order_ref, small_ref, router):
    rows = small_ref.shape[0]
    slot, row = iota((LANES, rows), 0), iota((LANES, rows), 1)
    chip = order_ref[order_ref.shape[0] - 1]
    fits = (row == (slot ^ chip) + 2) & (slot < experts)
    router[...] = dot(jnp.where(fits, 1.0, 0.0).astype(BF16), small_ref[...].astype(BF16)).astype(BF16)


def softmaxes(logits, places, experts):
    rows = iota(logits.shape, 0) < places
    lanes = iota(logits.shape, 1) < experts
    tall = jnp.where(rows, logits, LOW)
    tall = jnp.exp(tall - jnp.max(tall, axis=0, keepdims=True))
    dispatch = tall / jnp.sum(tall, axis=0, keepdims=True)
    wide = jnp.where(lanes, logits, LOW)
    wide = jnp.exp(wide - jnp.max(wide, axis=1, keepdims=True))
    combine = wide / jnp.sum(wide, axis=1, keepdims=True)
    return dispatch, combine


def route_body(
    places, experts, order_ref, token_ref, cot_ref, m0, m1, w_ref, small_ref,
    resid_ref, logit_ref, packed_ref, weight, router,
):
    @pl.when(pl.program_id(0) == 0)
    def _():
        place_rows(order_ref, w_ref, weight)
        spread_router(experts, order_ref, small_ref, router)

    resid = token_ref[0].astype(F32)
    part = m0.shape[-1]
    resid = resid + dot(m0[0], weight[:part, :]) + dot(m1[0], weight[part:, :])
    resid_ref[0] = resid
    normed, _ = normalize(resid)
    act = (normed * small_ref[1:2, :]).astype(BF16)
    logits = dot(act, router[...], NT)
    logit_ref[0] = logits
    dispatch, combine = softmaxes(logits, places, experts)
    features = act.shape[1]
    rows = packed_ref.shape[1]
    packed_ref[0, :, :features] = dot(dispatch.astype(BF16), act, TN)[:rows].astype(BF16)
    packed_ref[0, :, features:] = dot(combine.astype(BF16), cot_ref[0], TN)[:rows].astype(BF16)


def w_out_spec(w):
    features = w.shape[2] // 3
    return pl.BlockSpec(w.shape[:2] + (features,), lambda i: (0, 0, 2))


def route(places, experts, slot_rows, order, tokens, cot, mixed, w, small):
    images, tall, features = tokens.shape
    shapes = [
        ((images, tall, features), F32),
        ((images, tall, LANES), F32),
        ((images, slot_rows, 2 * features), BF16),
    ]
    return pl.pallas_call(
        functools.partial(route_body, places, experts),
        grid=(images,),
        in_specs=[SMEM, spec_image(tokens.shape), spec_image(cot.shape)]
        + [spec_image(m.shape) for m in mixed]
        + [w_out_spec(w), spec_whole(small.shape)],
        out_specs=[spec_image(s) for s, _ in shapes],
        out_shape=[jax.ShapeDtypeStruct(s, t) for s, t in shapes],
        scratch_shapes=[pltpu.VMEM((features, features), BF16), pltpu.VMEM((LANES, features), BF16)],
        compiler_params=params(),
        cost_estimate=cost(4 * images * tall * features * features, 8e6),
        name="route",
    )(order, tokens, cot, *mixed, w, small)


def gelu_parts(values):
    scale, cubic = 0.7978845608028654, 0.044715
    square = values * values
    bent = jnp.tanh(scale * values * (1.0 + cubic * square))
    half = 0.5 * (1.0 + bent)
    slope = half + 0.5 * values * (1.0 - bent * bent) * scale * (1.0 + 3.0 * cubic * square)
    return values * half, slope


def expert_body(rows_ref, in_ref, out_ref, back_ref):
    features = in_ref.shape[0]
    rows, arriving = rows_ref[:, :features], rows_ref[:, features:]
    total = jnp.zeros((rows.shape[0], features), F32)
    grad_total = total
    step = 512
    for start in range(0, in_ref.shape[1], step):
        w_in = in_ref[:, start : start + step]
        w_out = out_ref[start : start + step, :]
        hidden, slope = gelu_parts(dot(rows, w_in))
        grad_pre = (dot(arriving, w_out, NT) * slope).astype(BF16)
        total = total + dot(hidden.astype(BF16), w_out)
        grad_total = grad_total + dot(grad_pre, w_in, NT)
    back_ref[:, :features] = total.astype(BF16)
    back_ref[:, features:] = grad_total.astype(BF16)


def expert(rows, piece_in, piece_out):
    return pl.pallas_call(
        expert_body,
        grid=(1,),
        in_specs=[spec_whole(rows.shape), spec_whole(piece_in.shape), spec_whole(piece_out.shape)],
        out_specs=spec_whole(rows.shape),
        out_shape=jax.ShapeDtypeStruct(rows.shape, BF16),
        compiler_params=params(),
        cost_estimate=cost(8 * 256 * piece_in.size, 5e6),
        name="expert",
    )(rows, piece_in, piece_out)


def expert_grad_body(rows_ref, in_ref, out_ref, grad_in_ref, grad_out_ref):
    features = in_ref.shape[0]
    rows, arriving = rows_ref[:, :features], rows_ref[:, features:]
    hidden, slope = gelu_parts(dot(rows, in_ref[...]))
    grad_pre = (dot(arriving, out_ref[...], NT) * slope).astype(BF16)
    grad_in_ref[...] = dot(rows, grad_pre, TN)
    grad_out_ref[...] = dot(hidden.astype(BF16), arriving, TN)


def expert_grad(rows, piece_in, piece_out):
    features, hidden = piece_in.shape
    step = 512
    wide = pl.BlockSpec((features, step), lambda i: (0, i))
    high = pl.BlockSpec((step, features), lambda i: (i, 0))
    return pl.pallas_call(
        expert_grad_body,
        grid=(hidden // step,),
        in_specs=[spec_whole(rows.shape), wide, high],
        out_specs=[wide, high],
        out_shape=[
            jax.ShapeDtypeStruct(piece_in.shape, F32),
            jax.ShapeDtypeStruct(piece_out.shape, F32),
        ],
        compiler_params=params(),
        cost_estimate=cost(8 * rows.shape[0] * piece_in.size, 14e6),
        name="expert_grad",
    )(rows, piece_in, piece_out)


def back_body(
    places, experts, order_ref, resid_ref, logit_ref, cot_ref, m0, m1, summed_ref, w_ref, small_ref,
    output_ref, att_ref, grad_mixed_ref, grad_w_ref, grad_side_ref, weight, router_rows, slots, total, side, gain_sum,
):
    step = pl.program_id(0)
    features = small_ref.shape[1]

    @pl.when(step == 0)
    def _():
        place_rows(order_ref, w_ref, weight)
        spread_router(experts, order_ref, small_ref, router_rows)
        slots[...] = jnp.zeros_like(slots)
        total[...] = jnp.zeros_like(total)
        side[...] = jnp.zeros_like(side)
        gain_sum[...] = jnp.zeros_like(gain_sum)

    rows = summed_ref.shape[1]
    slots[:rows, :] = summed_ref[0]
    expert_sum, grad_slots = slots[:, :features], slots[:, features:]
    resid = resid_ref[0]
    cot = cot_ref[0]
    gain = small_ref[1:2, :]
    dispatch, combine = softmaxes(logit_ref[0], places, experts)
    output = resid + dot(combine.astype(BF16), expert_sum)
    output_ref[0] = output[:places].astype(BF16)
    normed, factor = normalize(resid)
    act = (normed * gain).astype(BF16)
    grad_comb = dot(cot, expert_sum, NT)
    grad_disp = dot(act, grad_slots, NT)
    grad_logits = combine * (grad_comb - jnp.sum(grad_comb * combine, axis=1, keepdims=True))
    grad_logits = grad_logits + dispatch * (
        grad_disp - jnp.sum(grad_disp * dispatch, axis=0, keepdims=True)
    )
    grad_logits = grad_logits.astype(BF16)
    grad_act = dot(dispatch.astype(BF16), grad_slots) + dot(grad_logits, router_rows[...])
    side[...] += dot(act, grad_logits, TN)
    gain_sum[...] += jnp.sum(grad_act * normed, axis=0, keepdims=True)
    att = (cot.astype(F32) + norm_back(grad_act * gain, normed, factor)).astype(BF16)
    att_ref[0] = att
    grad_mixed_ref[0] = dot(att, weight[...], NT).astype(BF16)
    part = m0.shape[-1]
    total[:part, :] += dot(m0[0], att, TN)
    total[part:, :] += dot(m1[0], att, TN)

    @pl.when(step == pl.num_programs(0) - 1)
    def _():
        turned = jnp.broadcast_to(gain_sum[...], (LANES, features)).T
        lane = iota((features, LANES), 1)
        slot = iota((LANES, LANES), 0)
        slot = jnp.where(slot < experts, slot ^ order_ref[order_ref.shape[0] - 1], slot)
        swapped = jnp.where(slot == iota((LANES, LANES), 1), 1.0, 0.0).astype(BF16)
        side[...] = jnp.where(lane == experts, turned, dot(side[...].astype(BF16), swapped))
        grad_w_ref[...] = total[...].astype(BF16)
        grad_side_ref[...] = side[...].astype(BF16)


def back(places, experts, order, resid, logits, cot, mixed, summed, w, small):
    images, tall, features = resid.shape
    shapes = [
        ((images, places, features), BF16),
        ((images, tall, features), BF16),
        ((images, tall, features), BF16),
    ]
    grads = [(features, features), (features, LANES)]
    return pl.pallas_call(
        functools.partial(back_body, places, experts),
        grid=(images,),
        in_specs=[SMEM, spec_image(resid.shape), spec_image(logits.shape), spec_image(cot.shape)]
        + [spec_image(m.shape) for m in mixed]
        + [spec_image(summed.shape)]
        + [w_out_spec(w), spec_whole(small.shape)],
        out_specs=[spec_image(s) for s, _ in shapes] + [spec_whole(s) for s in grads],
        out_shape=[jax.ShapeDtypeStruct(s, t) for s, t in shapes]
        + [jax.ShapeDtypeStruct(s, BF16) for s in grads],
        scratch_shapes=[
            pltpu.VMEM((features, features), BF16),
            pltpu.VMEM((LANES, features), BF16),
            pltpu.VMEM((LANES, 2 * features), BF16),
            pltpu.VMEM((features, features), F32),
            pltpu.VMEM((features, LANES), F32),
            pltpu.VMEM((1, features), F32),
        ],
        compiler_params=params(),
        cost_estimate=cost(8 * images * tall * features * features, 16e6),
        name="back",
    )(order, resid, logits, cot, *mixed, summed, w, small)


def attend_back_body(extra, offset, order_ref, joint_ref, prob_ref, grad_ref, mixed_ref, act_ref, *refs):
    more, (out_ref, keep_ref, give_ref, total) = refs[:extra], refs[extra:]
    step = pl.program_id(0)

    @pl.when(step == 0)
    def _():
        total[...] = jnp.zeros_like(total)

    tall, width = joint_ref.shape[1:]
    third = width // 3
    low = iota((tall, LANES), 1) < LANES // 2
    for pair in range(third // LANES):
        query, keys, values = (
            joint_ref[0, :, part * third + pair * LANES : part * third + (pair + 1) * LANES]
            for part in range(3)
        )
        grad = grad_ref[0, :, offset + pair * LANES : offset + (pair + 1) * LANES]
        product = grad.astype(F32) * mixed_ref[0, :, pair * LANES : (pair + 1) * LANES].astype(F32)
        grads = []
        for side in range(2):
            mine = low if side == 0 else ~low
            prob = prob_ref[0, 2 * pair + side]
            inner = jnp.sum(jnp.where(mine, product, 0.0), axis=1, keepdims=True)
            grad_prob = dot(jnp.where(mine, grad, 0), values, NT)
            grad_scores = (prob.astype(F32) * (grad_prob - inner) * 0.125).astype(BF16)
            grads.append(
                (dot(grad_scores, keys), dot(grad_scores, query, TN), dot(prob, grad, TN))
            )
        for part in range(3):
            joined = jnp.where(low, grads[0][part], grads[1][part]).astype(BF16)
            out_ref[0, :, part * third + pair * LANES : part * third + (pair + 1) * LANES] = joined
    total[...] += dot(act_ref[0], out_ref[0], TN)

    @pl.when(step == pl.num_programs(0) - 1)
    def _():
        store_blocks(order_ref, total, keep_ref, give_ref, slice(0, width))
        place = width
        for source in more:
            end = place + source.shape[1]
            store_blocks(order_ref, source, keep_ref, give_ref, slice(place, end))
            place = end


def attend_back(blocks, offset, order, joint, prob, grad_mixed, mixed, act, more=()):
    images, tall, width = joint.shape
    features = act.shape[-1]
    third = width // 3
    columns = width + sum(m.shape[1] for m in more)
    half = (blocks // 2, features // blocks, columns)
    return pl.pallas_call(
        functools.partial(attend_back_body, len(more), offset),
        grid=(images,),
        in_specs=[
            SMEM,
            spec_image(joint.shape),
            spec_image(prob.shape),
            spec_image(grad_mixed.shape),
            spec_image(mixed.shape),
            spec_image(act.shape),
        ]
        + [spec_whole(m.shape) for m in more],
        out_specs=[spec_image(joint.shape), spec_whole(half), spec_whole(half)],
        out_shape=[
            jax.ShapeDtypeStruct(joint.shape, BF16),
            jax.ShapeDtypeStruct(half, BF16),
            jax.ShapeDtypeStruct(half, BF16),
        ],
        scratch_shapes=[pltpu.VMEM((features, width), F32)],
        compiler_params=params(),
        cost_estimate=cost(2 * images * tall * features * width * 5, 16e6),
        name="attend_back",
    )(order, joint, prob, grad_mixed, mixed, act, *more)


def finish_body(places, order_ref, token_ref, att_ref, j0, j1, w0, w1, small_ref, out_ref, s0, s1):
    @pl.when(pl.program_id(0) == 0)
    def _():
        for source, target in ((w0, s0), (w1, s1)):
            place_rows(order_ref, source, target)

    grad_act = dot(j0[0], s0[...], NT) + dot(j1[0], s1[...], NT)
    normed, factor = normalize(token_ref[0].astype(F32))
    result = att_ref[0].astype(F32) + norm_back(grad_act * small_ref[0:1, :], normed, factor)
    out_ref[0] = result[:places].astype(BF16)


def finish(places, order, tokens, att, joints, weights, small):
    images, tall, features = tokens.shape
    shape = (images, places, features)
    return pl.pallas_call(
        functools.partial(finish_body, places),
        grid=(images,),
        in_specs=[SMEM, spec_image(tokens.shape), spec_image(att.shape)]
        + [spec_image(j.shape) for j in joints]
        + [
            pl.BlockSpec(w.shape[:2] + (j.shape[2],), lambda i: (0, 0, 0))
            for w, j in zip(weights, joints)
        ]
        + [spec_whole(small.shape)],
        out_specs=spec_image(shape),
        out_shape=jax.ShapeDtypeStruct(shape, BF16),
        scratch_shapes=[pltpu.VMEM((features, j.shape[-1]), BF16) for j in joints],
        compiler_params=params(),
        cost_estimate=cost(6 * images * tall * features * features, 12e6),
        name="finish",
    )(order, tokens, att, *joints, *weights, small)


def per_device(
    tokens, cotangent, heads_in, heads_out, slot_router, first_gain, second_gain, expert_in, expert_out
):
    images, places, features = tokens.shape
    experts = slot_router.shape[1]
    group = lax.axis_size("grp")
    reps = lax.axis_size("rep")
    me = lax.axis_index("grp")
    own_rows = heads_in.shape[0]
    chip = me // 2
    direct = group == 8
    blocks = 8
    ways = jnp.arange(blocks, dtype=jnp.int32)
    if direct:
        order = jnp.concatenate([ways ^ me, (ways % 4 * 2 + ways // 4) ^ me, chip[None]])
    else:
        order = jnp.concatenate([ways, ways, chip[None]])
    tall = -(-places // 16) * 16
    slot_rows = -(-experts // 16) * 16
    part = features // 3
    wide = 3 * part

    thirds = [heads_in[:, k * features : (k + 1) * features] for k in range(3)]
    head_part = jnp.concatenate([t[:, :part] for t in thirds], axis=1)
    tail_part = jnp.concatenate([t[:, part:] for t in thirds] + [heads_out], axis=1)
    small = jnp.concatenate([first_gain[None], second_gain[None], slot_router.T], axis=0)
    small_rows = -(-small.shape[0] // 16) * 16
    grow = ((0, 0), (0, tall - places), (0, 0))
    source = jnp.pad(tokens, grow)
    cot = jnp.pad(cotangent, grow)
    if direct:
        small = jnp.pad(small, ((0, small_rows - small.shape[0]), (0, wide - own_rows)))
        head_part = jnp.concatenate([head_part, small], axis=0)
        middle = head_part.shape[0] // 2
        half = own_rows // 2
        first = gather_stage(head_part[None, :middle], group, 2)
        second = gather_stage(head_part[None, middle:], group, 4)
        tail = after(tail_part, first, second)
        first = gather_stage(first, group, 4)
        second = gather_stage(second, group, 2)
        tail_first = gather_stage(tail[None, :half], group, 2)
        tail_second = gather_stage(tail[None, half:], group, 4)
        held = join_halves(first, second)
        w_head = jnp.stack([held, swap(held, "grp", group, 1)], axis=1)
        w_head = w_head.reshape(blocks, -1, wide)
        tail_first, tail_second, source, cot = after((tail_first, tail_second, source, cot), w_head)
        source = after(source, cot, tail_first, tail_second)
    else:
        w_head = lax.all_gather(head_part, "grp", axis=0, tiled=True).reshape(blocks, -1, wide)
        small = lax.all_gather(small, "grp", axis=1, tiled=True).reshape(-1, blocks, features // blocks)
        small = small.transpose(1, 0, 2)
        small = jnp.pad(
            small,
            ((0, 0), (0, small_rows - small.shape[1]), (0, wide - small.shape[2])),
        )
        w_head = jnp.concatenate([w_head, small], axis=1)
        w_tail = lax.all_gather(tail_part, "grp", axis=0, tiled=True).reshape(blocks, -1, 3 * features)

    act, small, joint_head, prob_head, mixed_head = attend(
        True, places, order, source, w_head, (wide, 0)
    )
    if direct:
        first = swap(tail_first, "grp", group, 4)
        second = swap(tail_second, "grp", group, 2)
        first, second = after((first, second), mixed_head)
        held = join_halves(
            jnp.concatenate([tail_first, first]), jnp.concatenate([tail_second, second])
        )
        w_tail = jnp.stack([held, swap(held, "grp", group, 1)], axis=1)
        w_tail = w_tail.reshape(blocks, -1, 3 * features)
    joint_tail, prob_tail, mixed_tail = attend(False, places, order, act, w_tail, (2 * wide, 0))
    mixes = [mixed_head, mixed_tail]
    resid, logits, packed = route(
        places, experts, slot_rows, order, source, cot, mixes, w_tail, small
    )

    leaving = packed[:, :experts].transpose(1, 0, 2)
    arrived = jnp.stack(
        [leaving[0]] + [swap(leaving[k], "grp", group, 2 * k) for k in range(1, experts)]
    )
    arrived = jnp.stack([arrived, swap(arrived, "grp", group, 1)])
    received = arrived.reshape(2 * experts * images, 2 * features)
    piece_in, piece_out = expert_in[0], expert_out[0]
    result = expert(received, piece_in, piece_out).reshape(2, experts, images, 2 * features)
    both = add_low(result[0], swap(result[1], "grp", group, 1))
    summed = jnp.stack(
        [both[0]] + [swap(both[k], "grp", group, 2 * k) for k in range(1, experts)], axis=1
    )
    summed = jnp.pad(summed, ((0, 0), (0, slot_rows - experts), (0, 0)))

    every = received
    every = jnp.concatenate([every, swap(after(every, summed), "rep", reps, 1)])
    output, att, grad_mixed, grad_out, grad_side = back(
        places, experts, order, resid, logits, cot, mixes, summed, w_tail, small
    )
    grad_mixed, every = lax.optimization_barrier((grad_mixed, every))
    far = swap(every, "rep", reps, 2)
    grad_joint_tail, keep_tail, give_tail = attend_back(
        blocks, part, order, joint_tail, prob_tail, grad_mixed, mixed_tail, act,
        (grad_out, grad_side),
    )
    if direct:
        own, others, sums = spread_sum(keep_tail, give_tail)
        grad_mixed = after(grad_mixed, *sums)
    grad_joint_head, keep_head, give_head = attend_back(
        blocks, 0, order, joint_head, prob_head, grad_mixed, mixed_head, act
    )
    every = jnp.concatenate([every, after(far, grad_joint_head)])
    if direct:
        own, others = after((own, others), grad_joint_head)
        tail_sum = add_low(own, *others)
        odd = lax.axis_index("rep") % 2 == 1
        upper, lower = tail_sum[:half], tail_sum[half:]
        mine = jnp.where(odd, lower, upper)
        other = swap(jnp.where(odd, upper, lower), "rep", reps, 1)
        own, others, sums = spread_sum(keep_head, give_head)
        att = after(att, mine, *sums)
        token_grad = finish(
            places, order, source, att, [grad_joint_head, grad_joint_tail], [w_head, w_tail], small
        )
        (own, others), other = after(((own, others), other), token_grad)
        tail_sum = add_low(mine, other)
        head_sum = add_low(own, *others)
        every, tail_sum, head_sum = after((every, tail_sum, head_sum), token_grad)
        tail_other = swap(tail_sum, "rep", reps, 2)
        head_other = swap(head_sum, "rep", reps, 1)
        expert_in_grad, expert_out_grad = expert_grad(every, piece_in, piece_out)
        tail_other, head_other = after((tail_other, head_other), expert_in_grad)
        tail_sum, head_sum = add_low(tail_sum, tail_other), add_low(head_sum, head_other)
        tail_other = swap(tail_sum, "rep", reps, 1)
        head_sum = head_sum.astype(F32) + swap(head_sum, "rep", reps, 3).astype(F32)
        tail_sum = jnp.concatenate(
            [jnp.where(odd, tail_other, tail_sum), jnp.where(odd, tail_sum, tail_other)]
        ).astype(F32)
    else:
        tail_sum = jnp.concatenate([keep_tail, give_tail]).reshape(features, -1)
        tail_sum = lax.psum_scatter(tail_sum, "grp", scatter_dimension=0, tiled=True)
        head_sum = jnp.concatenate([keep_head, give_head]).reshape(features, -1)
        head_sum = lax.psum_scatter(head_sum, "grp", scatter_dimension=0, tiled=True)
        token_grad = finish(
            places, order, source, att, [grad_joint_head, grad_joint_tail], [w_head, w_tail], small
        )
        expert_in_grad, expert_out_grad = expert_grad(every, piece_in, piece_out)
        tail_sum = lax.psum(tail_sum, "rep").astype(F32)
        head_sum = lax.psum(head_sum, "rep").astype(F32)

    pieces = []
    for k in range(3):
        pieces.append(head_sum[:, k * part : (k + 1) * part])
        pieces.append(tail_sum[:, 2 * k * part : 2 * (k + 1) * part])
    heads_in_sum = jnp.concatenate(pieces, axis=1)
    gain_one_grad = jnp.sum(heads_in_sum * heads_in.astype(F32), axis=1) / first_gain.astype(F32)
    rest = tail_sum[:, 2 * wide :]
    return (
        output,
        token_grad,
        heads_in_sum,
        rest[:, :features],
        rest[:, features : features + experts],
        gain_one_grad,
        rest[:, features + experts],
        expert_in_grad[None],
        expert_out_grad[None],
    )


def solution(mesh):
    token_spec = P(("rep", "grp"), None, None)
    matrix, vector, stack = P("grp", None), P("grp"), P("grp", None, None)
    return jax.shard_map(
        per_device,
        mesh=mesh,
        in_specs=(token_spec, token_spec, matrix, matrix, matrix, vector, vector, stack, stack),
        out_specs=(token_spec, token_spec, matrix, matrix, matrix, vector, vector, stack, stack),
        check_vma=False,
    )
```

time: 255 us -> 213 us (0.84)
  starting transfers between devices: 54.3 us -> 37.9 us
  Pallas kernels: 126 us -> 116 us
  local copies, waits for them, and re-layouts: 21.8 us -> 13.5 us
    ppermute x46 -> x33, starting transfers between devices: 49.2 us -> 37.9 us  [swap(): lax.ppermute(values, axis, [(place, place ^ bit) for place in range(size)])]
    slice x14 -> x6, local copies, waits for them, and re-layouts: 10.3 us -> 2.68 us  [the longest x1 1.01 us: per_device(): t[:, part:]]
    pallas_call x3 -> x2, Pallas kernels: 32.4 us -> 25.4 us  [attend(): pl.pallas_call(functools.partial(attend_body, first, places), grid=(image...]
    ppermute x3 -> x0, starting transfers between devices: 5.1 us -> none  [per_device(): lax.ppermute(received, 'rep', [(i, (i + k) % reps) for i in range(reps)])]
    reshape x6 -> x0, local copies, waits for them, and re-layouts: 2.98 us -> none  [the longest x1 1.55 us: per_device(): columns = heads_in.reshape(own_rows, 3, chunks, part)]
    another operation x19 -> x2, local copies, waits for them, and re-layouts: 0.73 us -> 3.31 us  [the longest x1 2.06 us: per_device(): w_tail = jnp.stack([held, swap(held, 'grp', group, 1)], axis=1)]
    pallas_call x3 -> x2, Pallas kernels: 39.8 us -> 37.5 us  [attend_back(): pl.pallas_call(functools.partial(attend_back_body, len(more), offset), gr...]
    ppermute x46 -> x33, waiting for transfers between devices: 36.1 us -> 33.8 us  [swap(): lax.ppermute(values, axis, [(place, place ^ bit) for place in range(size)])]
  transfers between devices with their start and end apart: 49 -> 33, of which waited for: 23 -> 16; matrix products, arithmetic and copies ran while one was open for 8% -> 5% of each run, Pallas kernels for 35% -> 29%
where the time goes in v1:
time: 213 us; the launch traced here: 212 us
  Pallas kernels  116 us (54%)
  starting transfers between devices  37.9 us (18%)
  waiting for transfers between devices  33.8 us (16%)
  local copies, waits for them, and re-layouts  13.5 us (6%)
  other arithmetic  9.78 us (5%)
    ppermute x33, starting transfers between devices, swap(): lax.ppermute(values, axis, [(place, place ^ bit) for place in range(size)])  37.9 us
    pallas_call x2, Pallas kernels, attend_back(): pl.pallas_call(functools.partial(attend_back_body, len(more), offset), gr...  37.5 us
    ppermute x33, waiting for transfers between devices, swap(): lax.ppermute(values, axis, [(place, place ^ bit) for place in range(size)])  33.8 us
    pallas_call x2, Pallas kernels, attend(): pl.pallas_call(functools.partial(attend_body, first, places), grid=(image...  25.4 us
    pallas_call x1, Pallas kernels, back(): pl.pallas_call(functools.partial(back_body, places, experts), grid=(image...  16.1 us
    pallas_call x1, Pallas kernels, finish(): pl.pallas_call(functools.partial(finish_body, places), grid=(images,), in...  12.8 us
    pallas_call x1, Pallas kernels, route(): pl.pallas_call(functools.partial(route_body, places, experts), grid=(imag...  11 us
    pallas_call x1, Pallas kernels, expert_grad(): pl.pallas_call(expert_grad_body, grid=(hidden // step,), in_specs=[spec_w...  7.97 us
  transfers between devices with their start and end apart: 33, of which 16 were waited for; matrix products, arithmetic and copies ran while one was open for 5% of the time, Pallas kernels for 29%

profile of v1, /device:TPU:0, one launch (start us, length us, event | category | flops | bytes accessed | tf_op | source)
XLA Modules:
  0.0 212.3 jit_solution(3244047675250613983)
XLA Ops:
  2.2 3.0 %collective-permute-start.1 = (bf16[1,56,768]{2,1,0:T(8,128)(2,1)S(1)}, bf16[1,56,768]{2,1,0:T(8,128)(2,1)S(1)}, u32[]{:S(2)}, u32[]{:S(2)}) collective-permute-start(bf16[1,56,768]{2,1,0:T(8,128)(2,1)S(1)} %get-tuple-element.186), channel_id=1, source_target_pairs={{0,4},{1,5},{2,6},{3,7},{4,0},{5,1},{6,2},{7,3},{8,12},{9,13},{10,... | collective-permute-start | bytes 258056 | tf_op jit(solution)/shard_map/ppermute | solution.py:27
  7.8 3.1 %pad.16.source_ref.token_ref = bf16[6,208,768]{2,1,0:T(8,128)(2,1)} pad(bf16[6,197,768]{2,1,0:T(8,128)(2,1)} %param.9, bf16[]{:T(256)} %constant.63.clone.1), padding=0_0x0_11x0_0 | pad | bytes 3732482 | tf_op jit(solution)/shard_map/jit(_pad)/pad | solution.py:578
  13.8 2.0 collective-permute-start.3
  17.3 3.1 %collective-permute-done.5 = bf16[2,56,768]{2,1,0:T(8,128)(2,1)S(1)} collective-permute-done((bf16[2,56,768]{2,1,0:T(8,128)(2,1)S(1)}, bf16[2,56,768]{2,1,0:T(8,128)(2,1)S(1)}, u32[]{:S(2)}, u32[]{:S(2)}) %collective-permute-start.5) | collective-permute-done | bytes 172064 | tf_op jit(solution)/shard_map/ppermute | solution.py:27
  21.2 2.5 %collective-permute-done.3 = bf16[1,48,2304]{2,1,0:T(8,128)(2,1)S(1)} collective-permute-done((bf16[1,48,2304]{2,1,0:T(8,128)(2,1)S(1)}, bf16[1,48,2304]{2,1,0:T(8,128)(2,1)S(1)}, u32[]{:S(2)}, u32[]{:S(2)}) %collective-permute-start.3) | collective-permute-done | bytes 221216 | tf_op jit(solution)/shard_map/ppermute | solution.py:27
  27.3 11.9 %attend.2 = (bf16[6,208,768]{2,1,0:T(8,128)(2,1)}, f32[16,768]{1,0:T(8,128)}, bf16[6,208,768]{2,1,0:T(8,128)(2,1)}, bf16[6,4,208,208]{3,2,1,0:T(8,128)(2,1)}, bf16[6,208,256]{2,1,0:T(8,128)(2,1)}) custom-call(s32[17]{0:T(128)} %pad_add_fusion.order_ref, bf16[6,208,768]{2,1,0:T(8,128)(2,1)} %pad.16.source_ref.token_ref, bf16[8,112,768]{2,1,0:T(8,128)(2,1)} %bitcast.72), custom_call_target="tpu_custom_call" | custom-call | flops 4416602112 | bytes 8000000 | tf_op jit(solution)/shard_map/attend/pallas_call | solution.py:198
  39.6 3.6 %collective-permute-done.9 = bf16[4,96,2304]{2,1,0:T(8,128)(2,1)S(1)} collective-permute-done((bf16[4,96,2304]{2,1,0:T(8,128)(2,1)S(1)}, bf16[4,96,2304]{2,1,0:T(8,128)(2,1)S(1)}, u32[]{:S(2)}, u32[]{:S(2)}) %collective-permute-start.9) | collective-permute-done | bytes 1769504 | tf_op jit(solution)/shard_map/ppermute | solution.py:27
  43.4 2.1 copy.50
  45.5 13.5 %attend.3 = (bf16[6,208,1536]{2,1,0:T(8,128)(2,1)}, bf16[6,8,208,208]{3,2,1,0:T(8,128)(2,1)}, bf16[6,208,512]{2,1,0:T(8,128)(2,1)}) custom-call(s32[17]{0:T(128)} %pad_add_fusion.order_ref, bf16[6,208,768]{2,1,0:T(8,128)(2,1)} %get-tuple-element.68.source_ref.act_ref, bf16[8,96,2304]{2,1,0:T(8,128)(2,1)} %bitcast.68), custom_call_target="tpu_custom_call" | custom-call | flops 8833204224 | bytes 8000000 | tf_op jit(solution)/shard_map/attend/pallas_call | solution.py:198
  59.0 11.0 %route.1 = (f32[6,208,768]{2,1,0:T(8,128)}, f32[6,208,128]{2,1,0:T(8,128)}, bf16[6,16,1536]{2,1,0:T(8,128)(2,1)}) custom-call(s32[17]{0:T(128)} %pad_add_fusion.order_ref, bf16[6,208,768]{2,1,0:T(8,128)(2,1)} %pad.16.source_ref.token_ref, bf16[6,208,768]{2,1,0:T(8,128)(2,1)} %pad.17.cot_ref, bf16[6,208,256]{2,1,0:T(8,128)(2,1)} %get-tuple-element.67.m0.mixed_ref, ...), custom_call_target="tpu_custom_call" | custom-call | flops 2944401408 | bytes 8000000 | tf_op jit(solution)/shard_map/route/pallas_call | solution.py:271
  75.4 2.5 %collective-permute-done.12 = bf16[6,1536]{1,0:T(8,128)(2,1)S(1)} collective-permute-done((bf16[6,1536]{1,0:T(8,128)(2,1)S(1)}, bf16[6,1536]{1,0:T(8,128)(2,1)S(1)}, u32[]{:S(2)}, u32[]{:S(2)}) %collective-permute-start.12) | collective-permute-done | bytes 18464 | tf_op jit(solution)/shard_map/ppermute | solution.py:27
  80.3 5.4 %expert.1 = bf16[48,1536]{1,0:T(8,128)(2,1)} custom-call(bf16[48,1536]{1,0:T(8,128)(2,1)} %reshape.68.rows_ref, bf16[768,1536]{1,0:T(8,128)(2,1)} %bitcast.89, bf16[1536,768]{1,0:T(8,128)(2,1)} %bitcast.91), custom_call_target="tpu_custom_call" | custom-call | flops 2415919104 | bytes 5000000 | tf_op jit(solution)/shard_map/expert/pallas_call | solution.py:313
  97.5 16.1 %back.1 = (bf16[6,197,768]{2,1,0:T(8,128)(2,1)}, bf16[6,208,768]{2,1,0:T(8,128)(2,1)}, bf16[6,208,768]{2,1,0:T(8,128)(2,1)}, bf16[768,768]{1,0:T(8,128)(2,1)}, bf16[768,128]{1,0:T(8,128)(2,1)}) custom-call(s32[17]{0:T(128)} %pad_add_fusion.order_ref, f32[6,208,768]{2,1,0:T(8,128)} %get-tuple-element.73.resid_ref, ...), custom_call_target="tpu_custom_call" | custom-call | flops 5888802816 | bytes 16000000 | tf_op jit(solution)/shard_map/back/pallas_call | solution.py:418
  113.7 24.2 %attend_back.2 = (bf16[6,208,1536]{2,1,0:T(8,128)(2,1)}, bf16[4,96,2432]{2,1,0:T(8,128)(2,1)}, bf16[4,96,2432]{2,1,0:T(8,128)(2,1)}) custom-call(s32[17]{0:T(128)} %pad_add_fusion.order_ref, bf16[6,208,1536]{2,1,0:T(8,128)(2,1)} %get-tuple-element.78.joint_ref, bf16[6,8,208,208]{3,2,1,0:T(8,128)(2,1)} %get-tuple-element.79.prob_ref, ...), custom_call_target="tpu_custom_call" | custom-call | flops 14722007040 | bytes 16000000 | tf_op jit(solution)/shard_map/attend_back/pallas_call | solution.py:491
  138.0 2.6 %collective-permute-start.24 = (bf16[96,1536]{1,0:T(8,128)(2,1)S(1)}, bf16[96,1536]{1,0:T(8,128)(2,1)S(1)}, u32[]{:S(2)}, u32[]{:S(2)}) collective-permute-start(bf16[96,1536]{1,0:T(8,128)(2,1)S(1)} %pad_maximum_fusion.6), channel_id=1, source_target_pairs={{0,16},{8,24},{16,0},{24,8},{1,17},{9,25},{17,1},{25,9},{2,18},{10... | collective-permute-start | bytes 884744 | tf_op jit(solution)/shard_map/ppermute | solution.py:27
  142.0 1.9 fusion.7
  147.4 13.3 %attend_back.3 = (bf16[6,208,768]{2,1,0:T(8,128)(2,1)}, bf16[4,96,768]{2,1,0:T(8,128)(2,1)}, bf16[4,96,768]{2,1,0:T(8,128)(2,1)}) custom-call(s32[17]{0:T(128)} %pad_add_fusion.order_ref, bf16[6,208,768]{2,1,0:T(8,128)(2,1)} %get-tuple-element.87.joint_ref, bf16[6,4,208,208]{3,2,1,0:T(8,128)(2,1)} %get-tuple-element.88.prob_ref, ...), custom_call_target="tpu_custom_call" | custom-call | flops 7361003520 | bytes 16000000 | tf_op jit(solution)/shard_map/attend_back/pallas_call | solution.py:491
  161.6 5.2 %collective-permute-done.21 = bf16[96,2432]{1,0:T(8,128)(2,1)S(1)} collective-permute-done((bf16[96,2432]{1,0:T(8,128)(2,1)S(1)}, bf16[96,2432]{1,0:T(8,128)(2,1)S(1)}, u32[]{:S(2)}, u32[]{:S(2)}) %collective-permute-start.21) | collective-permute-done | bytes 466976 | tf_op jit(solution)/shard_map/ppermute | solution.py:27
  171.3 12.8 %finish.1 = bf16[6,197,768]{2,1,0:T(8,128)(2,1)} custom-call(s32[17]{0:T(128)} %pad_add_fusion.order_ref, bf16[6,208,768]{2,1,0:T(8,128)(2,1)} %pad.16.source_ref.token_ref, bf16[6,208,768]{2,1,0:T(8,128)(2,1)} %get-tuple-element.97.att_ref, bf16[6,208,768]{2,1,0:T(8,128)(2,1)} %get-tuple-element.90.j0, bf16[6,208,1536]{2,1,0:T(8,128)(2,1)} %get-tuple-element.98.j1, ...), custom_call_target="tpu_custom_call" | custom-call | flops 4416602112 | bytes 12000000 | tf_op jit(solution)/shard_map/finish/pallas_call | solution.py:531
  184.3 2.8 %collective-permute-start.29 = (bf16[48,2432]{1,0:T(8,128)(2,1)S(1)}, bf16[48,2432]{1,0:T(8,128)(2,1)S(1)}, u32[]{:S(2)}, u32[]{:S(2)}) collective-permute-start(bf16[48,2432]{1,0:T(8,128)(2,1)S(1)} %add_convert_fusion.6), channel_id=1, source_target_pairs={{0,16},{8,24},{16,0},{24,8},{1,17},{9,25},{17,1},{25,9},{2,18},{10... | collective-permute-start | bytes 700424 | tf_op jit(solution)/shard_map/ppermute | solution.py:27
  188.6 8.0 %expert_grad.1 = (f32[768,1536]{1,0:T(8,128)}, f32[1536,768]{1,0:T(8,128)}) custom-call(bf16[192,1536]{1,0:T(8,128)(2,1)} %pad_maximum_fusion.2.rows_ref, bf16[768,1536]{1,0:T(8,128)(2,1)} %bitcast.90, bf16[1536,768]{1,0:T(8,128)(2,1)} %bitcast.92), custom_call_target="tpu_custom_call" | custom-call | flops 1811939328 | bytes 14000000 | tf_op jit(solution)/shard_map/expert_grad/pallas_call | solution.py:339
  196.7 3.3 %collective-permute-start.31 = (bf16[96,768]{1,0:T(8,128)(2,1)S(1)}, bf16[96,768]{1,0:T(8,128)(2,1)S(1)}, u32[]{:S(2)}, u32[]{:S(2)}) collective-permute-start(bf16[96,768]{1,0:T(8,128)(2,1)S(1)} %add_convert_fusion.7), channel_id=1, source_target_pairs={{0,24},{8,16},{16,8},{24,0},{1,25},{9,17},{17,9},{25,1},{2,26},{10... | collective-permute-start | bytes 442376 | tf_op jit(solution)/shard_map/ppermute | solution.py:27
  200.1 5.2 %collective-permute-done.31 = bf16[96,768]{1,0:T(8,128)(2,1)S(1)} collective-permute-done((bf16[96,768]{1,0:T(8,128)(2,1)S(1)}, bf16[96,768]{1,0:T(8,128)(2,1)S(1)}, u32[]{:S(2)}, u32[]{:S(2)}) %collective-permute-start.31) | collective-permute-done | bytes 147488 | tf_op jit(solution)/shard_map/ppermute | solution.py:27
  205.4 3.7 %collective-permute-done.32 = bf16[48,2432]{1,0:T(8,128)(2,1)S(1)} collective-permute-done((bf16[48,2432]{1,0:T(8,128)(2,1)S(1)}, bf16[48,2432]{1,0:T(8,128)(2,1)S(1)}, u32[]{:S(2)}, u32[]{:S(2)}) %collective-permute-start.32) | collective-permute-done | bytes 233504 | tf_op jit(solution)/shard_map/ppermute | solution.py:27
  (138 shorter events, 48.5 us)
Async XLA Ops:
  2.2 10.8 %collective-permute-start.1 = (bf16[1,56,768]{2,1,0:T(8,128)(2,1)S(1)}, bf16[1,56,768]{2,1,0:T(8,128)(2,1)S(1)}, u32[]{:S(2)}, u32[]{:S(2)}) collective-permute-start(bf16[1,56,768]{2,1,0:T(8,128)(2,1)S(1)} %get-tuple-element.186), channel_id=1, source_target_pairs={{0,4},{1,5},{2,6},{3,7},{4,0},{5,1},{6,2},{7,3},{8,12},{9,13},{10,... | collective-permute-start | bytes 258056 | tf_op jit(solution)/shard_map/ppermute | solution.py:27
  5.3 8.4 %collective-permute-start = (bf16[1,56,768]{2,1,0:T(8,128)(2,1)S(1)}, bf16[1,56,768]{2,1,0:T(8,128)(2,1)S(1)}, u32[]{:S(2)}, u32[]{:S(2)}) collective-permute-start(bf16[1,56,768]{2,1,0:T(8,128)(2,1)S(1)} %get-tuple-element.187), channel_id=1, source_target_pairs={{0,2},{1,3},{2,0},{3,1},{4,6},{5,7},{6,4},{7,5},{8,10},{9,11},{10,... | collective-permute-start | bytes 258056 | tf_op jit(solution)/shard_map/ppermute | solution.py:27
  13.0 7.4 %collective-permute-start.5 = (bf16[2,56,768]{2,1,0:T(8,128)(2,1)S(1)}, bf16[2,56,768]{2,1,0:T(8,128)(2,1)S(1)}, u32[]{:S(2)}, u32[]{:S(2)}) collective-permute-start(bf16[2,56,768]{2,1,0:T(8,128)(2,1)S(1)} %pad_maximum_fusion.8), channel_id=1, source_target_pairs={{0,2},{1,3},{2,0},{3,1},{4,6},{5,7},{6,4},{7,5},{8,10},{9,11},{10,... | collective-permute-start | bytes 516104 | tf_op jit(solution)/shard_map/ppermute | solution.py:27
  13.7 7.4 %collective-permute-start.4 = (bf16[2,56,768]{2,1,0:T(8,128)(2,1)S(1)}, bf16[2,56,768]{2,1,0:T(8,128)(2,1)S(1)}, u32[]{:S(2)}, u32[]{:S(2)}) collective-permute-start(bf16[2,56,768]{2,1,0:T(8,128)(2,1)S(1)} %pad_maximum_fusion.7), channel_id=1, source_target_pairs={{0,4},{1,5},{2,6},{3,7},{4,0},{5,1},{6,2},{7,3},{8,12},{9,13},{10,... | collective-permute-start | bytes 516104 | tf_op jit(solution)/shard_map/ppermute | solution.py:27
  13.8 9.9 %collective-permute-start.3 = (bf16[1,48,2304]{2,1,0:T(8,128)(2,1)S(1)}, bf16[1,48,2304]{2,1,0:T(8,128)(2,1)S(1)}, u32[]{:S(2)}, u32[]{:S(2)}) collective-permute-start(bf16[1,48,2304]{2,1,0:T(8,128)(2,1)S(1)} %get-tuple-element.174), channel_id=1, source_target_pairs={{0,4},{1,5},{2,6},{3,7},{4,0},{5,1},{6,2},{7,3},{8,12},{9,13},{10,... | collective-permute-start | bytes 663560 | tf_op jit(solution)/shard_map/ppermute | solution.py:27
  15.8 7.9 %collective-permute-start.2 = (bf16[1,48,2304]{2,1,0:T(8,128)(2,1)S(1)}, bf16[1,48,2304]{2,1,0:T(8,128)(2,1)S(1)}, u32[]{:S(2)}, u32[]{:S(2)}) collective-permute-start(bf16[1,48,2304]{2,1,0:T(8,128)(2,1)S(1)} %get-tuple-element.175), channel_id=1, source_target_pairs={{0,2},{1,3},{2,0},{3,1},{4,6},{5,7},{6,4},{7,5},{8,10},{9,11},{10,... | collective-permute-start | bytes 663560 | tf_op jit(solution)/shard_map/ppermute | solution.py:27
  25.2 13.9 %collective-permute-start.8 = (bf16[2,48,2304]{2,1,0:T(8,128)(2,1)S(1)}, bf16[2,48,2304]{2,1,0:T(8,128)(2,1)S(1)}, u32[]{:S(2)}, u32[]{:S(2)}) collective-permute-start(bf16[2,48,2304]{2,1,0:T(8,128)(2,1)S(1)} %pad_maximum_fusion.5), channel_id=1, source_target_pairs={{0,2},{1,3},{2,0},{3,1},{4,6},{5,7},{6,4},{7,5},{8,10},{9,11},{10,... | collective-permute-start | bytes 1327112 | tf_op jit(solution)/shard_map/ppermute | solution.py:27
  26.7 12.4 %collective-permute-start.7 = (bf16[2,48,2304]{2,1,0:T(8,128)(2,1)S(1)}, bf16[2,48,2304]{2,1,0:T(8,128)(2,1)S(1)}, u32[]{:S(2)}, u32[]{:S(2)}) collective-permute-start(bf16[2,48,2304]{2,1,0:T(8,128)(2,1)S(1)} %pad_maximum_fusion.4), channel_id=1, source_target_pairs={{0,4},{1,5},{2,6},{3,7},{4,0},{5,1},{6,2},{7,3},{8,12},{9,13},{10,... | collective-permute-start | bytes 1327112 | tf_op jit(solution)/shard_map/ppermute | solution.py:27
  73.2 4.7 %collective-permute-start.12 = (bf16[6,1536]{1,0:T(8,128)(2,1)S(1)}, bf16[6,1536]{1,0:T(8,128)(2,1)S(1)}, u32[]{:S(2)}, u32[]{:S(2)}) collective-permute-start(bf16[6,1536]{1,0:T(8,128)(2,1)S(1)} %bitcast.81), channel_id=1, source_target_pairs={{0,6},{1,7},{2,4},{3,5},{4,2},{5,3},{6,0},{7,1},{8,14},{9,15},{10,... | collective-permute-start | bytes 55304 | tf_op jit(solution)/shard_map/ppermute | solution.py:27
  88.1 4.8 %collective-permute-start.17 = (bf16[6,1536]{1,0:T(8,128)(2,1)S(1)}, bf16[6,1536]{1,0:T(8,128)(2,1)S(1)}, u32[]{:S(2)}, u32[]{:S(2)}) collective-permute-start(bf16[6,1536]{1,0:T(8,128)(2,1)S(1)} %get-tuple-element.189), channel_id=1, source_target_pairs={{0,6},{1,7},{2,4},{3,5},{4,2},{5,3},{6,0},{7,1},{8,14},{9,15},{10,... | collective-permute-start | bytes 55304 | tf_op jit(solution)/shard_map/ppermute | solution.py:27
  95.9 17.7 %collective-permute-start.18 = (bf16[48,1536]{1,0:T(8,128)(2,1)S(1)}, bf16[48,1536]{1,0:T(8,128)(2,1)S(1)}, u32[]{:S(2)}, u32[]{:S(2)}) collective-permute-start(bf16[48,1536]{1,0:T(8,128)(2,1)S(1)} %copy-done.4), channel_id=1, source_target_pairs={{0,8},{8,0},{16,24},{24,16},{1,9},{9,1},{17,25},{25,17},{2,10},{10... | collective-permute-start | bytes 442376 | tf_op jit(solution)/shard_map/ppermute | solution.py:27
  138.0 22.7 %collective-permute-start.24 = (bf16[96,1536]{1,0:T(8,128)(2,1)S(1)}, bf16[96,1536]{1,0:T(8,128)(2,1)S(1)}, u32[]{:S(2)}, u32[]{:S(2)}) collective-permute-start(bf16[96,1536]{1,0:T(8,128)(2,1)S(1)} %pad_maximum_fusion.6), channel_id=1, source_target_pairs={{0,16},{8,24},{16,0},{24,8},{1,17},{9,25},{17,1},{25,9},{2,18},{10... | collective-permute-start | bytes 884744 | tf_op jit(solution)/shard_map/ppermute | solution.py:27
  143.9 17.8 %collective-permute-start.22 = (bf16[96,2432]{1,0:T(8,128)(2,1)S(1)}, bf16[96,2432]{1,0:T(8,128)(2,1)S(1)}, u32[]{:S(2)}, u32[]{:S(2)}) collective-permute-start(bf16[96,2432]{1,0:T(8,128)(2,1)S(1)} %get-tuple-element.158), channel_id=1, source_target_pairs={{0,6},{1,7},{2,4},{3,5},{4,2},{5,3},{6,0},{7,1},{8,14},{9,15},{10,... | collective-permute-start | bytes 1400840 | tf_op jit(solution)/shard_map/ppermute | solution.py:27
  144.4 22.5 %collective-permute-start.21 = (bf16[96,2432]{1,0:T(8,128)(2,1)S(1)}, bf16[96,2432]{1,0:T(8,128)(2,1)S(1)}, u32[]{:S(2)}, u32[]{:S(2)}) collective-permute-start(bf16[96,2432]{1,0:T(8,128)(2,1)S(1)} %get-tuple-element.159), channel_id=1, source_target_pairs={{0,4},{1,5},{2,6},{3,7},{4,0},{5,1},{6,2},{7,3},{8,12},{9,13},{10,... | collective-permute-start | bytes 1400840 | tf_op jit(solution)/shard_map/ppermute | solution.py:27
  145.9 20.9 %collective-permute-start.20 = (bf16[96,2432]{1,0:T(8,128)(2,1)S(1)}, bf16[96,2432]{1,0:T(8,128)(2,1)S(1)}, u32[]{:S(2)}, u32[]{:S(2)}) collective-permute-start(bf16[96,2432]{1,0:T(8,128)(2,1)S(1)} %get-tuple-element.160), channel_id=1, source_target_pairs={{0,2},{1,3},{2,0},{3,1},{4,6},{5,7},{6,4},{7,5},{8,10},{9,11},{10,... | collective-permute-start | bytes 1400840 | tf_op jit(solution)/shard_map/ppermute | solution.py:27
  160.7 6.9 %collective-permute-start.23 = (bf16[4,96,768]{2,1,0:T(8,128)(2,1)}, bf16[4,96,768]{2,1,0:T(8,128)(2,1)S(1)}, u32[]{:S(2)}, u32[]{:S(2)}) collective-permute-start(bf16[4,96,768]{2,1,0:T(8,128)(2,1)} %get-tuple-element.96), channel_id=1, source_target_pairs={{0,1},{1,0},{2,3},{3,2},{4,5},{5,4},{6,7},{7,6},{8,9},{9,8},{10,11... | collective-permute-start | bytes 1769480 | tf_op jit(solution)/shard_map/ppermute | solution.py:27
  167.2 16.9 %collective-permute-start.28 = (bf16[48,2432]{1,0:T(8,128)(2,1)S(1)}, bf16[48,2432]{1,0:T(8,128)(2,1)S(1)}, u32[]{:S(2)}, u32[]{:S(2)}) collective-permute-start(bf16[48,2432]{1,0:T(8,128)(2,1)S(1)} %get-tuple-element.168), channel_id=1, source_target_pairs={{0,8},{8,0},{16,24},{24,16},{1,9},{9,1},{17,25},{25,17},{2,10},{10... | collective-permute-start | bytes 700424 | tf_op jit(solution)/shard_map/ppermute | solution.py:27
  167.8 16.3 %collective-permute-start.27 = (bf16[96,768]{1,0:T(8,128)(2,1)S(1)}, bf16[96,768]{1,0:T(8,128)(2,1)S(1)}, u32[]{:S(2)}, u32[]{:S(2)}) collective-permute-start(bf16[96,768]{1,0:T(8,128)(2,1)S(1)} %get-tuple-element.162), channel_id=1, source_target_pairs={{0,6},{1,7},{2,4},{3,5},{4,2},{5,3},{6,0},{7,1},{8,14},{9,15},{10,... | collective-permute-start | bytes 442376 | tf_op jit(solution)/shard_map/ppermute | solution.py:27
  169.2 14.9 %collective-permute-start.26 = (bf16[96,768]{1,0:T(8,128)(2,1)S(1)}, bf16[96,768]{1,0:T(8,128)(2,1)S(1)}, u32[]{:S(2)}, u32[]{:S(2)}) collective-permute-start(bf16[96,768]{1,0:T(8,128)(2,1)S(1)} %get-tuple-element.163), channel_id=1, source_target_pairs={{0,4},{1,5},{2,6},{3,7},{4,0},{5,1},{6,2},{7,3},{8,12},{9,13},{10,... | collective-permute-start | bytes 442376 | tf_op jit(solution)/shard_map/ppermute | solution.py:27
  170.7 13.5 %collective-permute-start.25 = (bf16[96,768]{1,0:T(8,128)(2,1)S(1)}, bf16[96,768]{1,0:T(8,128)(2,1)S(1)}, u32[]{:S(2)}, u32[]{:S(2)}) collective-permute-start(bf16[96,768]{1,0:T(8,128)(2,1)S(1)} %get-tuple-element.164), channel_id=1, source_target_pairs={{0,2},{1,3},{2,0},{3,1},{4,6},{5,7},{6,4},{7,5},{8,10},{9,11},{10,... | collective-permute-start | bytes 442376 | tf_op jit(solution)/shard_map/ppermute | solution.py:27
  184.3 12.3 %collective-permute-start.29 = (bf16[48,2432]{1,0:T(8,128)(2,1)S(1)}, bf16[48,2432]{1,0:T(8,128)(2,1)S(1)}, u32[]{:S(2)}, u32[]{:S(2)}) collective-permute-start(bf16[48,2432]{1,0:T(8,128)(2,1)S(1)} %add_convert_fusion.6), channel_id=1, source_target_pairs={{0,16},{8,24},{16,0},{24,8},{1,17},{9,25},{17,1},{25,9},{2,18},{10... | collective-permute-start | bytes 700424 | tf_op jit(solution)/shard_map/ppermute | solution.py:27
  187.1 9.6 %collective-permute-start.30 = (bf16[96,768]{1,0:T(8,128)(2,1)S(1)}, bf16[96,768]{1,0:T(8,128)(2,1)S(1)}, u32[]{:S(2)}, u32[]{:S(2)}) collective-permute-start(bf16[96,768]{1,0:T(8,128)(2,1)S(1)} %add_convert_fusion.8), channel_id=1, source_target_pairs={{0,8},{8,0},{16,24},{24,16},{1,9},{9,1},{17,25},{25,17},{2,10},{10... | collective-permute-start | bytes 442376 | tf_op jit(solution)/shard_map/ppermute | solution.py:27
  196.7 8.6 %collective-permute-start.31 = (bf16[96,768]{1,0:T(8,128)(2,1)S(1)}, bf16[96,768]{1,0:T(8,128)(2,1)S(1)}, u32[]{:S(2)}, u32[]{:S(2)}) collective-permute-start(bf16[96,768]{1,0:T(8,128)(2,1)S(1)} %add_convert_fusion.7), channel_id=1, source_target_pairs={{0,24},{8,16},{16,8},{24,0},{1,25},{9,17},{17,9},{25,1},{2,26},{10... | collective-permute-start | bytes 442376 | tf_op jit(solution)/shard_map/ppermute | solution.py:27
  200.0 9.0 %collective-permute-start.32 = (bf16[48,2432]{1,0:T(8,128)(2,1)S(1)}, bf16[48,2432]{1,0:T(8,128)(2,1)S(1)}, u32[]{:S(2)}, u32[]{:S(2)}) collective-permute-start(bf16[48,2432]{1,0:T(8,128)(2,1)S(1)} %add_convert_fusion.5), channel_id=1, source_target_pairs={{0,8},{8,0},{16,24},{24,16},{1,9},{9,1},{17,25},{25,17},{2,10},{10... | collective-permute-start | bytes 700424 | tf_op jit(solution)/shard_map/ppermute | solution.py:27
  (16 other events, 53.7 us)
